TPU v7x, 32 devices: a whole 2x2x4 slice. The times are simulated.
32 devices in a mesh: wide: 4 (over z), sec: 2 (over y), tile: 4 (over x, core).
Axes of the slice: x: 2, y: 2, z: 4, core: 2. Of those that a mesh axis runs over, the one named last changes fastest.
Arguments:
- velocity: float32 [3, 16, 64, 256], P(None, 'wide', 'tile', 'sec'), may hold values from -0.4 to 0.4
- viscosity: float32 [16, 64, 256], P('wide', 'tile', 'sec'), may hold values from 0.01 to 0.08
- counts: int32 [4, 2, 4], P('wide', 'sec', 'tile'), may hold values from 2 to 4, as said below
- destination: int32 [4, 2, 4, 4], P('wide', 'sec', 'tile'), may hold values from 0 to 3, as said below
- seeds: int32 [4, 2, 4, 4, 3, 128], P('wide', 'sec', 'tile'), may hold values from 0 to 127, as said below
- substeps: int32 [4, 2, 4, 4, 128], P('wide', 'sec', 'tile'), may hold values from 0 to 1
Outputs:
- new_velocity: float32 [3, 16, 64, 256], P(None, 'wide', 'tile', 'sec')
- traced_blocks: float32 [4, 2, 4, 8, 3, 128], P('wide', 'sec', 'tile')
Inputs may be any that keep to these rules, and one draw needn't show every extreme that they name: Blocks 0 to counts - 1 of a device are live; some device has all 4 live. `destination`: among a device's live blocks at most 2 name any one tile, and exactly 2 name the tile that all devices with the same wide and sec index share. `seeds`: components 0, 1, 2 lie below 4, 16, 128.
All inputs are finite; a program needn't handle non-finite values.
Results may differ from a plain program's by a relative error of at most 0.0003.
Values sent between devices are 32-bit elements; how exact they have to be, the bound alone decides.
A program may use at most 64 MiB of HBM per device.

v0:
```python
from functools import partial

import jax
import jax.numpy as jnp
from jax import lax
from jax.sharding import PartitionSpec as P

CAP = 2


flow_step = 0.2
trace_step = 1.25


def extended_2(block, sides, width):
    for axis, dim in sides:
        count = lax.axis_size(axis)
        forward = [(i, i + 1) for i in range(count - 1)]
        forward.append((count - 1, 0))
        backward = [(target, source) for source, target in forward]
        low = lax.ppermute(
            lax.slice_in_dim(block, block.shape[dim] - width, None, axis=dim), axis, forward
        )
        high = lax.ppermute(lax.slice_in_dim(block, 0, width, axis=dim), axis, backward)
        block = jnp.concatenate([low, block, high], axis=dim)
    return block


def neighbor(padded, dimension, offset):
    window = [slice(None), slice(1, -1), slice(1, -1), slice(1, -1)]
    length = padded.shape[dimension]
    window[dimension] = slice(1 + offset, length - 1 + offset)
    return padded[tuple(window)]


def advance(padded, viscous):
    centre = padded[:, 1:-1, 1:-1, 1:-1]
    spread = jnp.zeros_like(centre)
    laplace = jnp.zeros_like(centre)
    for component in range(3):
        dimension = component + 1
        upper_cell = neighbor(padded, dimension, 1)
        lower_cell = neighbor(padded, dimension, -1)
        flux_up = 0.25 * (centre + upper_cell) * (centre[component] + upper_cell[component])
        flux_down = 0.25 * (lower_cell + centre) * (lower_cell[component] + centre[component])
        spread = spread + (flux_up - flux_down)
        laplace = laplace + (upper_cell + lower_cell)
    laplace = laplace - 6.0 * centre
    return centre + flow_step * (viscous * laplace - spread)


def runge_kutta(offset, sampler):
    section_one = sampler(offset)
    section_two = sampler(0.5 * trace_step * section_one)
    section_three = sampler(0.5 * trace_step * section_two)
    section_four = sampler(trace_step * section_three)
    return trace_step / 6.0 * (section_one + 2.0 * section_two + 2.0 * section_three + section_four)


def march(offset, steps_float, sampler):
    moved_off = runge_kutta(offset, sampler)
    offset = jnp.where(0 < steps_float, moved_off, offset)
    return offset


def local_sampler(table, size_y, size_z, corner_base, box_offset, cells, offset):
    lowest = jnp.floor(offset)
    fraction = offset - lowest
    corner = cells + lowest.astype(jnp.int32) - corner_base
    linear_list = []
    weight_list = []
    for step_x in range(2):
        weight_x = fraction[0] if step_x else 1.0 - fraction[0]
        for step_y in range(2):
            weight_y = fraction[1] if step_y else 1.0 - fraction[1]
            for step_z in range(2):
                weight_z = fraction[2] if step_z else 1.0 - fraction[2]
                linear = (
                    ((corner[0] + step_x) * size_y + corner[1] + step_y) * size_z
                    + corner[2]
                    + step_z
                    + box_offset
                )
                linear_list.append(linear)
                weight_list.append(weight_x * weight_y * weight_z)
    linear_all = jnp.stack(linear_list)
    weight_all = jnp.stack(weight_list)
    point_total = offset.shape[1]
    values = jnp.take(table, linear_all.reshape(-1), axis=1).reshape(3, 8, point_total)
    return jnp.sum(values * weight_all[None], 1)


def wall_mask(field, depth, rows_y, tile_pos, total_y):
    global_rows = tile_pos * rows_y + jnp.arange(rows_y + 2 * depth, dtype=jnp.int32) - depth
    keeping = (global_rows >= 0) & (global_rows < total_y)
    return jnp.where(keeping[None, None, :, None], field, 0.0)


def shards(velocity, viscosity, counts, destination, seeds, substeps):
    rows_x = velocity.shape[1]
    rows_y = velocity.shape[2]
    rows_z = velocity.shape[3]
    tile_count = lax.axis_size("tile")
    tile_pos = lax.axis_index("tile")
    wide_pos = lax.axis_index("wide")
    sec_pos = lax.axis_index("sec")
    total_y = rows_y * tile_count
    padded = extended_2(velocity, (("wide", 1), ("sec", 3), ("tile", 2)), 1)
    padded = wall_mask(padded, 1, rows_y, tile_pos, total_y)
    fresh_vel = advance(padded, viscosity)
    extended = extended_2(fresh_vel, (("wide", 1), ("sec", 3), ("tile", 2)), 1)
    extended = wall_mask(extended, 1, rows_y, tile_pos, total_y)
    size_y = rows_y + 2
    size_z = rows_z + 2
    box_cells = (rows_x + 2) * size_y * size_z
    block_count = destination.shape[3]
    point_count = seeds.shape[5]
    is_live = jnp.arange(block_count, dtype=jnp.int32) < counts[0, 0, 0]
    target = destination[0, 0, 0]
    onehot = (
        (target[:, None] == jnp.arange(tile_count, dtype=jnp.int32)[None, :]) & is_live[:, None]
    ).astype(jnp.int32)
    order_rank = jnp.sum(onehot * (jnp.cumsum(onehot, 0) - onehot), 1)
    slot_count = CAP * tile_count
    slot_index = target * CAP + order_rank
    placing = (
        (slot_index[None, :] == jnp.arange(slot_count, dtype=jnp.int32)[:, None]) & is_live[None, :]
    ).astype(jnp.float32)
    anchor = jnp.stack(
        [
            jnp.full_like(target, wide_pos * rows_x),
            target * rows_y,
            jnp.full_like(target, sec_pos * rows_z),
        ],
        1,
    )
    start_cell = seeds[0, 0, 0] + anchor[:, :, None]
    steps_float = substeps[0, 0, 0].astype(jnp.float32)
    tile_boxes = lax.all_gather(extended[None], "tile", axis=0, tiled=True)
    table = jnp.transpose(tile_boxes, (1, 0, 2, 3, 4)).reshape(3, -1)
    cells = jnp.transpose(start_cell, (1, 0, 2)).reshape(3, -1)
    per_point = jnp.repeat(target, point_count)
    corner_base = jnp.stack(
        [
            jnp.full_like(per_point, wide_pos * rows_x - 1),
            per_point * rows_y - 1,
            jnp.full_like(per_point, sec_pos * rows_z - 1),
        ]
    )
    box_offset = per_point * box_cells
    offset = jnp.zeros(cells.shape, jnp.float32)
    traced = march(
        offset,
        steps_float.reshape(-1),
        partial(local_sampler, table, size_y, size_z, corner_base, box_offset, cells),
    )
    traced = jnp.transpose(traced.reshape(3, block_count, point_count), (1, 0, 2))
    sending = jnp.dot(
        placing,
        traced.reshape(block_count, -1),
        precision=lax.Precision.HIGHEST,
        preferred_element_type=jnp.float32,
    )
    sending = sending.reshape(tile_count, CAP, 3, point_count)
    arrived = lax.all_to_all(sending, "tile", split_axis=0, concat_axis=0, tiled=True)
    result = arrived.reshape(slot_count, 3, point_count)
    return (fresh_vel, result[None, None, None])


def solution(mesh):
    in_specs = (
        P(None, "wide", "tile", "sec"),
        P("wide", "tile", "sec"),
        P("wide", "sec", "tile"),
        P("wide", "sec", "tile", None),
        P("wide", "sec", "tile", None, None, None),
        P("wide", "sec", "tile", None, None),
    )
    out_specs = (P(None, "wide", "tile", "sec"), P("wide", "sec", "tile", None, None, None))
    return jax.shard_map(shards, mesh=mesh, in_specs=in_specs, out_specs=out_specs, check_vma=False)
```

profile of v0, /device:TPU:0, one launch (start us, length us, event | category | flops | bytes accessed | tf_op | source)
XLA Modules:
  0.0 187.7 jit_solution(2225590562868371861)
XLA Ops:
  0.6 0.8 fusion.71
  1.4 5.0 %collective-permute-start.1 = (f32[3,1,16,128]{3,2,1,0:T(8,128)S(1)}, f32[3,1,16,128]{3,2,1,0:T(8,128)S(1)}, u32[]{:S(2)}, u32[]{:S(2)}) collective-permute-start(f32[3,1,16,128]{3,2,1,0:T(8,128)S(1)} %get-tuple-element.27), channel_id=1, source_target_pairs={{8,0},{16,8},{24,16},{0,24},{9,1},{17,9},{25,17},{1,25},{10,2},{18... | collective-permute-start | bytes 73736 | tf_op jit(solution)/shard_map/ppermute | solution.py:24
  7.9 0.7 fusion.31
  8.7 0.8 select_reduce_fusion
  10.3 0.8 fusion.25
  12.1 0.9 constant_dynamic-update-slice_fusion.1
  13.1 1.6 collective-permute-start.2
  15.2 4.2 %collective-permute-done.2 = f32[3,6,16,1]{3,2,1,0:T(8,128)S(1)} collective-permute-done((f32[3,6,16,1]{3,2,1,0:T(8,128)S(1)}, f32[3,6,16,1]{3,2,1,0:T(8,128)S(1)}, u32[]{:S(2)}, u32[]{:S(2)}) %collective-permute-start.2) | collective-permute-done | bytes 1184 | tf_op jit(solution)/shard_map/ppermute | solution.py:21
  19.4 1.6 collective-permute-done.3
  21.2 1.7 collective-permute-start.5
  23.0 1.4 collective-permute-done.4
  25.2 3.8 %collective-permute-start.7 = (f32[3,1,16,128]{3,2,1,0:T(8,128)S(1)}, f32[3,1,16,128]{3,2,1,0:T(8,128)S(1)}, u32[]{:S(2)}, u32[]{:S(2)}) collective-permute-start(f32[3,1,16,128]{3,2,1,0:T(8,128)S(1)} %get-tuple-element.26), channel_id=1, source_target_pairs={{8,0},{16,8},{24,16},{0,24},{9,1},{17,9},{25,17},{1,25},{10,2},{18... | collective-permute-start | bytes 73736 | tf_op jit(solution)/shard_map/ppermute | solution.py:24
  29.0 1.7 collective-permute-done.6
  30.9 1.6 collective-permute-start.8
  33.1 4.6 %collective-permute-done.8 = f32[3,6,16,1]{3,2,1,0:T(8,128)S(1)} collective-permute-done((f32[3,6,16,1]{3,2,1,0:T(8,128)S(1)}, f32[3,6,16,1]{3,2,1,0:T(8,128)S(1)}, u32[]{:S(2)}, u32[]{:S(2)}) %collective-permute-start.8) | collective-permute-done | bytes 1184 | tf_op jit(solution)/shard_map/ppermute | solution.py:21
  37.6 2.7 %collective-permute-done.9 = f32[3,6,16,1]{3,2,1,0:T(8,128)S(1)} collective-permute-done((f32[3,6,16,1]{3,2,1,0:T(8,128)S(1)}, f32[3,6,16,1]{3,2,1,0:T(8,128)S(1)}, u32[]{:S(2)}, u32[]{:S(2)}) %collective-permute-start.9) | collective-permute-done | bytes 1184 | tf_op jit(solution)/shard_map/ppermute | solution.py:24
  40.6 1.7 collective-permute-start.11
  42.5 1.3 collective-permute-done.10
  43.9 14.3 %all_gather.3 = f32[4,3,6,18,130]{4,3,2,1,0:T(8,128)S(1)} all-gather(f32[1,3,6,18,130]{4,3,2,1,0:T(8,128)S(1)} %maximum_select_fusion.1), channel_id=1, replica_groups=mesh['wide'=4,'sec'=2,'tile'=4] {'tile'}, dimensions={0}, use_global_device_ids=true | all-gather | bytes 842400 | tf_op jit(solution)/shard_map/all_gather | solution.py:139
  58.4 1.2 reshape.248
  59.6 13.7 %copy.381 = f32[3,56160]{0,1:T(8,128)} copy(f32[3,56160]{1,0:T(4,128)S(1)} %reshape.248) | data formatting | bytes 1347840 | tf_op jit(solution)/shard_map/reshape | solution.py:140
  73.3 19.9 %gather_fusion = f32[4096,3]{1,0:T(8,128)S(1)} fusion(f32[3,56160]{0,1:T(8,128)} %copy.381, s32[4096]{0:T(1024)S(1)} %fusion.12), kind=kCustom, calls=%fused_computation.clone | custom fusion | bytes 114688 | tf_op jit(solution)/shard_map/jit(_take)/gather | solution.py:89
  93.3 2.1 %broadcast_select_fusion.3 = f32[4096,3]{1,0:T(8,128)S(1)} fusion(f32[4096,3]{1,0:T(8,128)S(1)} %gather_fusion, pred[4096]{0:T(1024)(128)(4,1)S(1)} %compare_and_fusion.3), kind=kLoop, calls=%fused_computation.11 | loop fusion | flops 12288 | bytes 102400 | tf_op jit(solution)/shard_map/jit(_take)/select_n | solution.py:89
  95.4 0.7 multiply_reduce_fusion.3
  96.5 23.4 %gather_fusion.1 = f32[4096,3]{1,0:T(8,128)} fusion(f32[3,56160]{0,1:T(8,128)} %copy.381, s32[4096]{0:T(1024)S(1)} %fusion.13), kind=kCustom, calls=%fused_computation.1.clone | custom fusion | bytes 114688 | tf_op jit(solution)/shard_map/jit(_take)/gather | solution.py:89
  119.9 3.6 %broadcast_select_fusion.2 = f32[4096,3]{1,0:T(8,128)S(1)} fusion(f32[4096,3]{1,0:T(8,128)} %gather_fusion.1, pred[4096]{0:T(1024)(128)(4,1)S(1)} %compare_and_fusion.2), kind=kLoop, calls=%fused_computation.10 | loop fusion | flops 12288 | bytes 102400 | tf_op jit(solution)/shard_map/jit(_take)/select_n | solution.py:89
  124.7 23.4 %gather_fusion.2 = f32[4096,3]{1,0:T(8,128)} fusion(f32[3,56160]{0,1:T(8,128)} %copy.381, s32[4096]{0:T(1024)S(1)} %fusion.14), kind=kCustom, calls=%fused_computation.2.clone | custom fusion | bytes 114688 | tf_op jit(solution)/shard_map/jit(_take)/gather | solution.py:89
  148.0 3.6 %broadcast_select_fusion.1 = f32[4096,3]{1,0:T(8,128)S(1)} fusion(f32[4096,3]{1,0:T(8,128)} %gather_fusion.2, pred[4096]{0:T(1024)(128)(4,1)S(1)} %compare_and_fusion.1), kind=kLoop, calls=%fused_computation.9 | loop fusion | flops 12288 | bytes 102400 | tf_op jit(solution)/shard_map/jit(_take)/select_n | solution.py:89
  151.7 0.7 multiply_reduce_fusion.1
  152.8 23.4 %gather_fusion.3 = f32[4096,3]{1,0:T(8,128)} fusion(f32[3,56160]{0,1:T(8,128)} %copy.381, s32[4096]{0:T(1024)S(1)} %fusion.15), kind=kCustom, calls=%fused_computation.3.clone | custom fusion | bytes 114688 | tf_op jit(solution)/shard_map/jit(_take)/gather | solution.py:89
  176.2 3.6 %broadcast_select_fusion = f32[4096,3]{1,0:T(8,128)S(1)} fusion(f32[4096,3]{1,0:T(8,128)} %gather_fusion.3, pred[4096]{0:T(1024)(128)(4,1)S(1)} %compare_and_fusion), kind=kLoop, calls=%fused_computation.8 | loop fusion | flops 12288 | bytes 102400 | tf_op jit(solution)/shard_map/jit(_take)/select_n | solution.py:89
  180.9 6.2 %all_to_all.5 = f32[4,2,3,128]{3,1,2,0:T(2,128)S(1)} all-to-all(f32[4,2,3,128]{3,1,2,0:T(2,128)S(1)} %fusion.22), channel_id=1, replica_groups=mesh['wide'=4,'sec'=2,'tile'=4] {'tile'}, dimensions={0} | all-to-all | bytes 24576 | tf_op jit(solution)/shard_map/all_to_all | solution.py:165
  (99 shorter events, 9.1 us)
Async XLA Ops:
  0.6 24.2 %copy-start.1 = (f32[4,16,128]{2,1,0:T(8,128)S(1)}, f32[4,16,128]{2,1,0:T(8,128)}, u32[]{:S(2)}) copy-start(f32[4,16,128]{2,1,0:T(8,128)} %param.9) | copy-start | bytes 98308
  1.4 11.6 %collective-permute-start.1 = (f32[3,1,16,128]{3,2,1,0:T(8,128)S(1)}, f32[3,1,16,128]{3,2,1,0:T(8,128)S(1)}, u32[]{:S(2)}, u32[]{:S(2)}) collective-permute-start(f32[3,1,16,128]{3,2,1,0:T(8,128)S(1)} %get-tuple-element.27), channel_id=1, source_target_pairs={{8,0},{16,8},{24,16},{0,24},{9,1},{17,9},{25,17},{1,25},{10,2},{18... | collective-permute-start | bytes 73736 | tf_op jit(solution)/shard_map/ppermute | solution.py:24
  6.5 5.6 %collective-permute-start = (f32[3,1,16,128]{3,2,1,0:T(8,128)S(1)}, f32[3,1,16,128]{3,2,1,0:T(8,128)S(1)}, u32[]{:S(2)}, u32[]{:S(2)}) collective-permute-start(f32[3,1,16,128]{3,2,1,0:T(8,128)S(1)} %get-tuple-element.28), channel_id=1, source_target_pairs={{0,8},{8,16},{16,24},{24,0},{1,9},{9,17},{17,25},{25,1},{2,10},{10... | collective-permute-start | bytes 73736 | tf_op jit(solution)/shard_map/ppermute | solution.py:21
  13.1 19.9 %copy-start.2 = (s32[1,1,1,4,128]{4,3,2,1,0:T(4,128)S(1)}, s32[1,1,1,4,128]{4,3,2,1,0:T(4,128)}, u32[]{:S(2)}) copy-start(s32[1,1,1,4,128]{4,3,2,1,0:T(4,128)} %param.13) | copy-start | bytes 6148
  13.1 6.3 %collective-permute-start.2 = (f32[3,6,16,1]{3,2,1,0:T(8,128)S(1)}, f32[3,6,16,1]{3,2,1,0:T(8,128)S(1)}, u32[]{:S(2)}, u32[]{:S(2)}) collective-permute-start(f32[3,6,16,1]{3,2,1,0:T(8,128)S(1)} %get-tuple-element.23), channel_id=1, source_target_pairs={{0,4},{4,0},{1,5},{5,1},{2,6},{6,2},{3,7},{7,3},{8,12},{12,8},{9,1... | collective-permute-start | bytes 3464 | tf_op jit(solution)/shard_map/ppermute | solution.py:21
  14.7 6.3 %collective-permute-start.3 = (f32[3,6,16,1]{3,2,1,0:T(8,128)S(1)}, f32[3,6,16,1]{3,2,1,0:T(8,128)S(1)}, u32[]{:S(2)}, u32[]{:S(2)}) collective-permute-start(f32[3,6,16,1]{3,2,1,0:T(8,128)S(1)} %get-tuple-element.24), channel_id=1, source_target_pairs={{4,0},{0,4},{5,1},{1,5},{6,2},{2,6},{7,3},{3,7},{12,8},{8,12},{13,... | collective-permute-start | bytes 3464 | tf_op jit(solution)/shard_map/ppermute | solution.py:24
  21.2 3.2 %collective-permute-start.4 = (f32[3,6,1,130]{3,2,1,0:T(1,128)S(1)}, f32[3,6,1,130]{3,2,1,0:T(1,128)S(1)}, u32[]{:S(2)}, u32[]{:S(2)}) collective-permute-start(f32[3,6,1,130]{3,2,1,0:T(1,128)S(1)} %get-tuple-element.17), channel_id=1, source_target_pairs={{0,1},{1,2},{2,3},{3,0},{4,5},{5,6},{6,7},{7,4},{8,9},{9,10},{10,1... | collective-permute-start | bytes 28088 | tf_op jit(solution)/shard_map/ppermute | solution.py:21
  21.2 3.2 %collective-permute-start.5 = (f32[3,6,1,130]{3,2,1,0:T(1,128)S(1)}, f32[3,6,1,130]{3,2,1,0:T(1,128)S(1)}, u32[]{:S(2)}, u32[]{:S(2)}) collective-permute-start(f32[3,6,1,130]{3,2,1,0:T(1,128)S(1)} %get-tuple-element.18), channel_id=1, source_target_pairs={{1,0},{2,1},{3,2},{0,3},{5,4},{6,5},{7,6},{4,7},{9,8},{10,9},{11,1... | collective-permute-start | bytes 28088 | tf_op jit(solution)/shard_map/ppermute | solution.py:24
  25.1 33.2 %copy-start = (f32[3,4,16,128]{3,2,1,0:T(8,128)}, f32[3,4,16,128]{3,2,1,0:T(8,128)S(1)}, u32[]{:S(2)}) copy-start(f32[3,4,16,128]{3,2,1,0:T(8,128)S(1)} %multiply_add_fusion) | copy-start | bytes 294916
  25.1 5.7 %collective-permute-start.6 = (f32[3,1,16,128]{3,2,1,0:T(8,128)S(1)}, f32[3,1,16,128]{3,2,1,0:T(8,128)S(1)}, u32[]{:S(2)}, u32[]{:S(2)}) collective-permute-start(f32[3,1,16,128]{3,2,1,0:T(8,128)S(1)} %get-tuple-element.25), channel_id=1, source_target_pairs={{0,8},{8,16},{16,24},{24,0},{1,9},{9,17},{17,25},{25,1},{2,10},{10... | collective-permute-start | bytes 73736 | tf_op jit(solution)/shard_map/ppermute | solution.py:21
  25.2 5.6 %collective-permute-start.7 = (f32[3,1,16,128]{3,2,1,0:T(8,128)S(1)}, f32[3,1,16,128]{3,2,1,0:T(8,128)S(1)}, u32[]{:S(2)}, u32[]{:S(2)}) collective-permute-start(f32[3,1,16,128]{3,2,1,0:T(8,128)S(1)} %get-tuple-element.26), channel_id=1, source_target_pairs={{8,0},{16,8},{24,16},{0,24},{9,1},{17,9},{25,17},{1,25},{10,2},{18... | collective-permute-start | bytes 73736 | tf_op jit(solution)/shard_map/ppermute | solution.py:24
  30.9 6.7 %collective-permute-start.8 = (f32[3,6,16,1]{3,2,1,0:T(8,128)S(1)}, f32[3,6,16,1]{3,2,1,0:T(8,128)S(1)}, u32[]{:S(2)}, u32[]{:S(2)}) collective-permute-start(f32[3,6,16,1]{3,2,1,0:T(8,128)S(1)} %get-tuple-element.21), channel_id=1, source_target_pairs={{0,4},{4,0},{1,5},{5,1},{2,6},{6,2},{3,7},{7,3},{8,12},{12,8},{9,1... | collective-permute-start | bytes 3464 | tf_op jit(solution)/shard_map/ppermute | solution.py:21
  32.5 7.8 %collective-permute-start.9 = (f32[3,6,16,1]{3,2,1,0:T(8,128)S(1)}, f32[3,6,16,1]{3,2,1,0:T(8,128)S(1)}, u32[]{:S(2)}, u32[]{:S(2)}) collective-permute-start(f32[3,6,16,1]{3,2,1,0:T(8,128)S(1)} %get-tuple-element.22), channel_id=1, source_target_pairs={{4,0},{0,4},{5,1},{1,5},{6,2},{2,6},{7,3},{3,7},{12,8},{8,12},{13,... | collective-permute-start | bytes 3464 | tf_op jit(solution)/shard_map/ppermute | solution.py:24
  40.5 3.2 %collective-permute-start.10 = (f32[3,6,1,130]{3,2,1,0:T(1,128)S(1)}, f32[3,6,1,130]{3,2,1,0:T(1,128)S(1)}, u32[]{:S(2)}, u32[]{:S(2)}) collective-permute-start(f32[3,6,1,130]{3,2,1,0:T(1,128)S(1)} %get-tuple-element.19), channel_id=1, source_target_pairs={{0,1},{1,2},{2,3},{3,0},{4,5},{5,6},{6,7},{7,4},{8,9},{9,10},{10,1... | collective-permute-start | bytes 28088 | tf_op jit(solution)/shard_map/ppermute | solution.py:21
  40.6 3.2 %collective-permute-start.11 = (f32[3,6,1,130]{3,2,1,0:T(1,128)S(1)}, f32[3,6,1,130]{3,2,1,0:T(1,128)S(1)}, u32[]{:S(2)}, u32[]{:S(2)}) collective-permute-start(f32[3,6,1,130]{3,2,1,0:T(1,128)S(1)} %get-tuple-element.20), channel_id=1, source_target_pairs={{1,0},{2,1},{3,2},{0,3},{5,4},{6,5},{7,6},{4,7},{9,8},{10,9},{11,1... | collective-permute-start | bytes 28088 | tf_op jit(solution)/shard_map/ppermute | solution.py:24
where the time goes:
time: 188 us
  local copies, waits for them, and re-layouts  109 us (58%)
  other arithmetic  21.6 us (11%)
  blocking collectives  20.5 us (11%)
  waiting for transfers between devices  18.2 us (10%)
  starting transfers between devices  16.7 us (9%)
    gather x4, local copies, waits for them, and re-layouts, local_sampler(): jnp.take(table, linear_all.reshape(-1), axis=1).reshape(3, 8, point_total)  90.1 us
    reshape x2, local copies, waits for them, and re-layouts, shards(): table = jnp.transpose(tile_boxes, (1, 0, 2, 3, 4)).reshape(3, -1)  14.9 us
    all_gather x1, blocking collectives, shards(): tile_boxes = lax.all_gather(extended[None], 'tile', axis=0, tiled=True)  14.3 us
    ppermute x6, waiting for transfers between devices, extended_2(): lax.ppermute(lax.slice_in_dim(block, block.shape[dim] - width, None, axis...  13.8 us
    ppermute x6, starting transfers between devices, extended_2(): lax.ppermute(lax.slice_in_dim(block, 0, width, axis=dim), axis, backward)  13.3 us
    select_n x4, other arithmetic, local_sampler(): jnp.take(table, linear_all.reshape(-1), axis=1).reshape(3, 8, point_total)  13 us
    all_to_all x1, blocking collectives, shards(): lax.all_to_all(sending, 'tile', split_axis=0, concat_axis=0, tiled=True)  6.18 us
    ppermute x6, waiting for transfers between devices, extended_2(): lax.ppermute(lax.slice_in_dim(block, 0, width, axis=dim), axis, backward)  4.33 us
  transfers between devices with their start and end apart: 12, of which 8 were waited for; matrix products, arithmetic and copies ran while one was open for 3% of the time, Pallas kernels for 0%

commit v1 on v0

v1 whole, which is shorter than its diff:
```python
import functools

import jax
import jax.numpy as jnp
from jax import lax
from jax.experimental import pallas as pl
from jax.experimental.pallas import tpu as pltpu
from jax.sharding import PartitionSpec as P

CAP = 2
SUB = 8
LANE = 128

flow_step = 0.2
trace_step = 1.25

MESH = pl.DeviceIdType.MESH


def plan(sizes):
    n_wide, n_sec, n_tile = sizes
    sides = (1,) if n_sec == 2 else (1, -1)
    rows = [("row", dx, dy, 0) for dx in (-1, 0, 1) for dy in (-1, 1)]
    cols = [("col", dx, dy, dz) for dz in sides for dx in (-1, 0, 1) for dy in (-1, 0, 1)]
    planes = [("plane", dx, 0, 0) for dx in (-1, 1)] + [("visc", dx, 0, 0) for dx in (-1, 1)]
    seeds = [("seed", 0, dy, 0) for dy in range(1, n_tile)]
    return sides, cols, rows, planes, seeds


def kernel(
    sizes,
    counts_ref, dest_ref, vel_ref, visc_ref, seeds_ref, steps_ref,
    new_ref, out_ref,
    ext, shifted, dense, col_out, row_out, col_mid, col_edge, row_in, seed_out, seed_in,
    send_sem, recv_sem,
):
    n_wide, n_sec, n_tile = sizes
    _, X, Y, Z = vel_ref.shape
    YE, ZE = Y + SUB, Z + LANE
    w, s, t = lax.axis_index("wide"), lax.axis_index("sec"), lax.axis_index("tile")
    sides, cols, rows, planes, seeds = plan(sizes)
    messages = seeds + cols + rows + planes

    def device(dx, dy, dz):
        return (
            lax.rem(w + (dx + n_wide), n_wide),
            lax.rem(s + (dz + n_sec), n_sec),
            lax.rem(t + (dy + n_tile), n_tile),
        )

    peers = sorted({(dx % n_wide, dy % n_tile, dz % n_sec) for _, dx, dy, dz in messages})
    barrier = pltpu.get_barrier_semaphore()
    for peer in peers:
        pl.semaphore_signal(barrier, inc=1, device_id=device(*peer), device_id_type=MESH)

    n_blk = seeds_ref.shape[0]
    count = counts_ref[0]
    target = [jnp.where(b < count, dest_ref[b], -1) for b in range(n_blk)]
    rank = []
    for b in range(n_blk):
        r = jnp.int32(0)
        for a in range(b):
            r = r + jnp.where(target[a] == target[b], 1, 0)
        rank.append(r)
    for d in range(n_tile):
        for r in range(CAP):
            cell = jnp.zeros((3, LANE), jnp.int32)
            step = jnp.zeros((1, LANE), jnp.int32)
            for b in range(n_blk):
                hit = jnp.where((target[b] == d) & (rank[b] == r), 1, 0)
                cell = cell + seeds_ref[b] * hit
                step = step + steps_ref[b : b + 1] * hit
            seed_out[d, 4 * r : 4 * r + 3] = cell
            seed_out[d, 4 * r + 3 : 4 * r + 4] = step

    lane = lax.broadcasted_iota(jnp.int32, (Y, LANE), 1)
    packed = jnp.zeros((Y, LANE), jnp.float32)
    for c in range(4):
        for x in range(X):
            k = c * X + x
            plane = vel_ref[c, x] if c < 3 else visc_ref[x]
            if Z == LANE:
                edge = plane
            else:
                edge = jnp.where(lane < LANE // 2, plane[:, :LANE], plane[:, Z - LANE :])
            moved = pltpu.roll(edge, (4 * k + 2) % LANE, 1)
            packed = jnp.where((lane >= 4 * k) & (lane < 4 * k + 4), moved, packed)
            row_out[0, 2 * k : 2 * k + 2] = plane[0:2]
            row_out[1, 2 * k : 2 * k + 2] = plane[Y - 2 : Y]
    col_out[...] = packed

    pl.semaphore_wait(barrier, len(peers))

    copies = {}
    for m, (kind, dx, dy, dz) in enumerate(messages):
        if kind == "seed":
            src, dst = seed_out.at[lax.rem(t + dy, n_tile)], seed_in.at[t]
        elif kind == "col":
            at = (sides.index(dz), dx + 1)
            if dy == 0:
                src, dst = col_out, col_mid.at[at]
            elif dy == 1:
                src, dst = col_out.at[Y - SUB : Y], col_edge.at[at + (0,)]
            else:
                src, dst = col_out.at[0:SUB], col_edge.at[at + (1,)]
        elif kind == "row":
            src, dst = row_out.at[1 if dy == 1 else 0], row_in.at[0 if dy == 1 else 1, dx + 1]
        elif kind == "plane":
            if dx == 1:
                src, dst = vel_ref.at[:, X - 2 : X], ext.at[0:3, 0:2, 0:Y, 0:Z]
            else:
                src, dst = vel_ref.at[:, 0:2], ext.at[0:3, X + 2 : X + 4, 0:Y, 0:Z]
        else:
            if dx == 1:
                src, dst = visc_ref.at[X - 1], ext.at[3, 1, 0:Y, 0:Z]
            else:
                src, dst = visc_ref.at[0], ext.at[3, X + 2, 0:Y, 0:Z]
        copy = pltpu.make_async_remote_copy(
            src_ref=src, dst_ref=dst, send_sem=send_sem.at[m], recv_sem=recv_sem.at[m],
            device_id=device(dx, dy, dz), device_id_type=MESH,
        )
        copy.start()
        copies[kind, dx, dy, dz] = copy

    seed_in[t] = seed_out[t]
    ext[0:3, 2 : X + 2, 0:Y, 0:Z] = vel_ref[...]
    ext[3, 2 : X + 2, 0:Y, 0:Z] = visc_ref[...]

    low_open = t > 0
    high_open = t < n_tile - 1
    spans = {0: [(x, x + 2) for x in range(X)], 1: [(X - 2, 0), (X - 1, 1)], -1: [(0, X + 2), (1, X + 3)]}

    for message in rows:
        copies[message].wait_recv()
    gap = jnp.zeros((SUB - 4, Z), jnp.float32)
    for dx in (-1, 0, 1):
        for c in range(4):
            for x, here in spans[dx]:
                if c == 3 and here in (0, X + 3):
                    continue
                k = c * X + x
                high = jnp.where(high_open, row_in[1, dx + 1, 2 * k : 2 * k + 2], 0.0)
                low = jnp.where(low_open, row_in[0, dx + 1, 2 * k : 2 * k + 2], 0.0)
                ext[c, here, Y:YE, 0:Z] = jnp.concatenate([high, gap, low], 0)

    for message in cols:
        copies[message].wait_recv()
    sub8 = lax.broadcasted_iota(jnp.int32, (SUB, LANE), 0)
    keep8 = ((sub8 < SUB // 2) & high_open) | ((sub8 >= SUB // 2) & low_open)
    for dx in (-1, 0, 1):
        whole = []
        for side in range(len(sides)):
            edge = jnp.where(sub8 < SUB // 2, col_edge[side, dx + 1, 1], col_edge[side, dx + 1, 0])
            edge = jnp.where(keep8, edge, 0.0)
            whole.append(jnp.concatenate([col_mid[side, dx + 1], edge], 0))
        if len(sides) == 2:
            lane_e = lax.broadcasted_iota(jnp.int32, (YE, LANE), 1)
            whole = jnp.where(lane_e % 4 < 2, whole[0], whole[1])
        else:
            whole = whole[0]
        for c in range(4):
            for x, here in spans[dx]:
                if c == 3 and here in (0, X + 3):
                    continue
                k = c * X + x
                ext[c, here, :, Z:ZE] = pltpu.roll(whole, LANE - 4 * k - 2, 1)

    for message in planes:
        copies[message].wait_recv()

    row = lax.broadcasted_iota(jnp.int32, (YE, ZE), 0)
    keep = (row < Y) | ((row < Y + SUB // 2) & high_open) | ((row >= Y + SUB // 2) & low_open)

    def flow(i, carry):
        u = [ext[c, i + 1] for c in range(3)]
        before = [ext[c, i] for c in range(3)]
        after = [ext[c, i + 2] for c in range(3)]
        viscous = ext[3, i + 1]
        up = [[pltpu.roll(u[c], length - 1, axis) for c in range(3)] for axis, length in ((0, YE), (1, ZE))]
        for c in range(3):
            spread = (u[c] + after[c]) * (u[0] + after[0]) - (before[c] + u[c]) * (before[0] + u[0])
            laplace = after[c] + before[c]
            for axis in range(2):
                face = (u[c] + up[axis][c]) * (u[axis + 1] + up[axis][axis + 1])
                spread = spread + (face - pltpu.roll(face, 1, axis))
                laplace = laplace + (up[axis][c] + pltpu.roll(u[c], 1, axis))
            laplace = laplace - 6.0 * u[c]
            fresh = u[c] + flow_step * (viscous * laplace - 0.25 * spread)
            fresh = jnp.where(keep, fresh, 0.0)
            for dz in range(3):
                along = fresh if dz == 1 else pltpu.roll(fresh, 1 if dz == 0 else ZE - 1, 1)
                along = along[:, 0:Z]
                for dy in range(3):
                    moved = along if dy == 1 else pltpu.roll(along, 1 if dy == 0 else YE - 1, 0)
                    shifted[dy, dz, c, i] = moved[0:Y]
        return carry

    lax.fori_loop(0, X + 2, flow, 0)

    def hat(e):
        return (jnp.maximum(-e, 0.0), 1.0 - jnp.abs(e), jnp.maximum(e, 0.0))

    def trace(i, carry):
        def sample(e):
            wx, wy, wz = hat(e[0]), hat(e[1]), hat(e[2])
            result = []
            for c in range(3):
                total = None
                for dx in range(3):
                    in_x = None
                    for dy in range(3):
                        in_y = None
                        for dz in range(3):
                            term = wz[dz] * shifted[dy, dz, c, i + dx]
                            in_y = term if in_y is None else in_y + term
                        term = wy[dy] * in_y
                        in_x = term if in_x is None else in_x + term
                    term = wx[dx] * in_x
                    total = term if total is None else total + term
                result.append(total)
            return result

        k1 = [shifted[1, 1, c, i + 1] for c in range(3)]
        k2 = sample([0.5 * trace_step * k for k in k1])
        k3 = sample([0.5 * trace_step * k for k in k2])
        k4 = sample([trace_step * k for k in k3])
        for c in range(3):
            new_ref[c, i] = k1[c]
            dense[c, i] = trace_step / 6.0 * (k1[c] + 2.0 * k2[c] + 2.0 * k3[c] + k4[c])
        return carry

    lax.fori_loop(0, X, trace, 0)

    for message in seeds:
        copies[message].wait_recv()

    sub = lax.broadcasted_iota(jnp.int32, (SUB, LANE), 0)
    for d in range(n_tile):
        for r in range(CAP):
            points = [jnp.broadcast_to(seed_in[d, 4 * r + j : 4 * r + j + 1], (SUB, LANE)) for j in range(4)]
            line = points[0] * Y + points[1]
            for c in range(3):
                found = jnp.zeros((SUB, LANE), jnp.float32)
                for x in range(X):
                    for y in range(0, Y, SUB):
                        for z in range(0, Z, LANE):
                            value = jnp.take_along_axis(
                                dense[c, x, y : y + SUB, z : z + LANE], points[2] & (LANE - 1), axis=1
                            )
                            hit = (line == x * Y + y + sub) & (points[3] > 0)
                            if Z > LANE:
                                hit = hit & (points[2] >= z) & (points[2] < z + LANE)
                            found = jnp.where(hit, value, found)
                out_ref[d * CAP + r, c : c + 1] = jnp.sum(found, 0, keepdims=True)

    for message in messages:
        copies[message].wait_send()


def shards(sizes, velocity, viscosity, counts, destination, seeds, substeps):
    _, X, Y, Z = velocity.shape
    n_wide, n_sec, n_tile = sizes
    n_blk, _, n_pts = seeds.shape[3:]
    sides, cols, rows, planes, seed_msgs = plan(sizes)
    total = len(cols) + len(rows) + len(planes) + len(seed_msgs)
    vmem = pl.BlockSpec(memory_space=pltpu.VMEM)
    smem = pl.BlockSpec(memory_space=pltpu.SMEM)
    f32 = jnp.float32
    row_total = -(-8 * X // SUB) * SUB
    fresh, result = pl.pallas_call(
        functools.partial(kernel, sizes),
        out_shape=(
            jax.ShapeDtypeStruct((3, X, Y, Z), f32),
            jax.ShapeDtypeStruct((n_tile * CAP, 3, n_pts), f32),
        ),
        in_specs=[smem, smem, vmem, vmem, vmem, vmem],
        out_specs=(vmem, vmem),
        scratch_shapes=[
            pltpu.VMEM((4, X + 4, Y + SUB, Z + LANE), f32),
            pltpu.VMEM((3, 3, 3, X + 2, Y, Z), f32),
            pltpu.VMEM((3, X, Y, Z), f32),
            pltpu.VMEM((Y, LANE), f32),
            pltpu.VMEM((2, row_total, Z), f32),
            pltpu.VMEM((len(sides), 3, Y, LANE), f32),
            pltpu.VMEM((len(sides), 3, 2, SUB, LANE), f32),
            pltpu.VMEM((2, 3, row_total, Z), f32),
            pltpu.VMEM((n_tile, 4 * CAP, n_pts), jnp.int32),
            pltpu.VMEM((n_tile, 4 * CAP, n_pts), jnp.int32),
            pltpu.SemaphoreType.DMA((total,)),
            pltpu.SemaphoreType.DMA((total,)),
        ],
        compiler_params=pltpu.CompilerParams(
            collective_id=0, has_side_effects=True, vmem_limit_bytes=16 * 2**20
        ),
    )(
        counts.reshape(1), destination.reshape(n_blk), velocity, viscosity,
        seeds.reshape(n_blk, 3, n_pts), substeps.reshape(n_blk, n_pts),
    )
    return fresh, result[None, None, None]


def solution(mesh):
    sizes = tuple(mesh.shape[axis] for axis in ("wide", "sec", "tile"))
    in_specs = (
        P(None, "wide", "tile", "sec"),
        P("wide", "tile", "sec"),
        P("wide", "sec", "tile"),
        P("wide", "sec", "tile", None),
        P("wide", "sec", "tile", None, None, None),
        P("wide", "sec", "tile", None, None),
    )
    out_specs = (P(None, "wide", "tile", "sec"), P("wide", "sec", "tile", None, None, None))
    return jax.shard_map(
        functools.partial(shards, sizes), mesh=mesh, in_specs=in_specs, out_specs=out_specs, check_vma=False
    )
```

time: 188 us -> 22 us (0.12)
  local copies, waits for them, and re-layouts: 109 us -> 3.59 us
  other arithmetic: 21.6 us -> 0 us
  blocking collectives: 20.5 us -> 0 us
  waiting for transfers between devices: 18.2 us -> 0 us
  Pallas kernels: 0 us -> 16.8 us
  starting transfers between devices: 16.7 us -> 0 us
    gather x4 -> x0, local copies, waits for them, and re-layouts: 90.1 us -> none  [local_sampler(): jnp.take(table, linear_all.reshape(-1), axis=1).reshape(3, 8, point_total)]
    ppermute x12 -> x0, waiting for transfers between devices: 18.2 us -> none  [the longest x6 13.8 us: extended_2(): lax.ppermute(lax.slice_in_dim(block, block.shape[dim] - width, None, axis...]
    pallas_call x0 -> x1, Pallas kernels: none -> 16.8 us  [shards(): pl.pallas_call(functools.partial(kernel, sizes), out_shape=(jax.ShapeDtyp...]
    ppermute x12 -> x0, starting transfers between devices: 16.7 us -> none  [the longest x6 13.3 us: extended_2(): lax.ppermute(lax.slice_in_dim(block, 0, width, axis=dim), axis, backward)]
    reshape x2 -> x0, local copies, waits for them, and re-layouts: 14.9 us -> none  [shards(): table = jnp.transpose(tile_boxes, (1, 0, 2, 3, 4)).reshape(3, -1)]
    all_gather x1 -> x0, blocking collectives: 14.3 us -> none  [shards(): tile_boxes = lax.all_gather(extended[None], 'tile', axis=0, tiled=True)]
    select_n x6 -> x0, other arithmetic: 13.3 us -> none  [the longest x4 13 us: local_sampler(): jnp.take(table, linear_all.reshape(-1), axis=1).reshape(3, 8, point_total)]
    all_to_all x1 -> x0, blocking collectives: 6.18 us -> none  [shards(): lax.all_to_all(sending, 'tile', split_axis=0, concat_axis=0, tiled=True)]
  transfers between devices with their start and end apart: 12 -> 0, of which waited for: 8 -> 0; matrix products, arithmetic and copies ran while one was open for 3% -> 0% of each run, Pallas kernels for 0% -> 0%
where the time goes in v1:
time: 22 us; the launch traced here: 21.7 us
  Pallas kernels  16.8 us (76%)
  local copies, waits for them, and re-layouts  3.59 us (16%)
  between operations  1.32 us (6%)
    pallas_call x1, Pallas kernels, shards(): pl.pallas_call(functools.partial(kernel, sizes), out_shape=(jax.ShapeDtyp...  16.8 us
    unnamed x13, local copies, waits for them, and re-layouts  3.59 us

profile of v1, /device:TPU:0, one launch (start us, length us, event | category | flops | bytes accessed | tf_op | source)
XLA Modules:
  0.0 21.7 jit_solution(11305575002355853424)
XLA Ops:
  0.6 0.0 copy-start.4
  1.3 0.0 copy-done.4
  1.3 0.0 copy-start.2
  1.3 0.0 copy-start.3
  1.3 0.7 %copy-done.2 = s32[1,1,1,4,128]{4,3,2,1,0:T(4,128)S(1)} copy-done((s32[1,1,1,4,128]{4,3,2,1,0:T(4,128)S(1)}, s32[1,1,1,4,128]{4,3,2,1,0:T(4,128)}, u32[]{:S(2)}) %copy-start.2) | copy-done | bytes 2072
  2.0 0.0 copy-done.3
  2.0 0.0 copy-start
  2.0 0.9 %copy-done = f32[3,4,16,128]{3,2,1,0:T(8,128)S(1)} copy-done((f32[3,4,16,128]{3,2,1,0:T(8,128)S(1)}, f32[3,4,16,128]{3,2,1,0:T(8,128)}, u32[]{:S(2)}) %copy-start) | copy-done | bytes 98328
  2.9 0.0 copy-start.1
  2.9 0.8 %copy-done.1 = f32[4,16,128]{2,1,0:T(8,128)S(1)} copy-done((f32[4,16,128]{2,1,0:T(8,128)S(1)}, f32[4,16,128]{2,1,0:T(8,128)}, u32[]{:S(2)}) %copy-start.1) | copy-done | bytes 32792
  3.7 16.8 %shard_map.77 = (f32[3,4,16,128]{3,2,1,0:T(8,128)S(1)}, f32[8,3,128]{2,1,0:T(4,128)S(1)}) custom-call(s32[1]{0:T(128)} %bitcast.7.counts_ref, s32[4]{0:T(128)S(1)} %bitcast.11, f32[3,4,16,128]{3,2,1,0:T(8,128)S(1)} %copy-done, f32[4,16,128]{2,1,0:T(8,128)S(1)} %copy-done.1, s32[4,3,128]{2,1,0:T(4,128)S(1)} %bitcast.8, s32[4,128]{1,0:T(4,128)S(1)} %bitcast.10), custom_call_target="tpu_custom_call" | custom-call | tf_op jit(solution)/shard_map/pallas_call | solution.py:270
  20.5 0.6 %copy.9 = f32[1,1,1,8,3,128]{5,3,4,2,1,0:T(8,128)} copy(f32[1,1,1,8,3,128]{5,4,3,2,1,0:T(4,128)S(1)} %bitcast.9) | data formatting | bytes 24576
  21.1 0.6 %copy.14 = f32[3,4,16,128]{3,2,1,0:T(8,128)} copy(f32[3,4,16,128]{3,2,1,0:T(8,128)S(1)} %get-tuple-element.10) | data formatting | bytes 196608
  (1 shorter events, 0.0 us)
Async XLA Ops:
  0.6 0.7 %copy-start.4 = (s32[1,1,1,4,3,128]{5,3,4,2,1,0:T(4,128)S(1)}, s32[1,1,1,4,3,128]{5,3,4,2,1,0:T(4,128)}, u32[]{:S(2)}) copy-start(s32[1,1,1,4,3,128]{5,3,4,2,1,0:T(4,128)} %param.10) | copy-start | bytes 18436
  1.3 0.7 %copy-start.2 = (s32[1,1,1,4,128]{4,3,2,1,0:T(4,128)S(1)}, s32[1,1,1,4,128]{4,3,2,1,0:T(4,128)}, u32[]{:S(2)}) copy-start(s32[1,1,1,4,128]{4,3,2,1,0:T(4,128)} %param.11) | copy-start | bytes 6148
  1.3 0.7 %copy-start.3 = (s32[1,1,1,4]{3,2,1,0:T(1,128)S(1)}, s32[1,1,1,4]{3,2,1,0:T(1,128)}, u32[]{:S(2)}) copy-start(s32[1,1,1,4]{3,2,1,0:T(1,128)} %param.9) | copy-start | bytes 52
  2.0 0.9 %copy-start = (f32[3,4,16,128]{3,2,1,0:T(8,128)S(1)}, f32[3,4,16,128]{3,2,1,0:T(8,128)}, u32[]{:S(2)}) copy-start(f32[3,4,16,128]{3,2,1,0:T(8,128)} %vel_ref.1) | copy-start | bytes 294916
  2.9 0.8 %copy-start.1 = (f32[4,16,128]{2,1,0:T(8,128)S(1)}, f32[4,16,128]{2,1,0:T(8,128)}, u32[]{:S(2)}) copy-start(f32[4,16,128]{2,1,0:T(8,128)} %visc_ref.1) | copy-start | bytes 98308

commit v2 on v1

--- a/solution.py
+++ b/solution.py
@@ -27,19 +27,22 @@
     return sides, cols, rows, planes, seeds
 
 
-def kernel(
+def exchange(
     sizes,
-    counts_ref, dest_ref, vel_ref, visc_ref, seeds_ref, steps_ref,
-    new_ref, out_ref,
-    ext, shifted, dense, col_out, row_out, col_mid, col_edge, row_in, seed_out, seed_in,
-    send_sem, recv_sem,
+    counts_ref, dest_hbm, vel_hbm, visc_hbm, seeds_hbm, steps_hbm,
+    shifted, seed_all,
+    ext, dest_ref, seeds_ref, steps_ref,
+    col_out, row_out, col_mid, col_edge, row_in, seed_out, seed_in,
+    send_sem, recv_sem, load_sem,
 ):
     n_wide, n_sec, n_tile = sizes
-    _, X, Y, Z = vel_ref.shape
+    _, X, Y, Z = vel_hbm.shape
     YE, ZE = Y + SUB, Z + LANE
     w, s, t = lax.axis_index("wide"), lax.axis_index("sec"), lax.axis_index("tile")
     sides, cols, rows, planes, seeds = plan(sizes)
-    messages = seeds + cols + rows + planes
+    messages = planes + cols + rows + seeds
+    low_open = t > 0
+    high_open = t < n_tile - 1
 
     def device(dx, dy, dz):
         return (
@@ -53,32 +56,26 @@
     for peer in peers:
         pl.semaphore_signal(barrier, inc=1, device_id=device(*peer), device_id_type=MESH)
 
-    n_blk = seeds_ref.shape[0]
-    count = counts_ref[0]
-    target = [jnp.where(b < count, dest_ref[b], -1) for b in range(n_blk)]
-    rank = []
-    for b in range(n_blk):
-        r = jnp.int32(0)
-        for a in range(b):
-            r = r + jnp.where(target[a] == target[b], 1, 0)
-        rank.append(r)
-    for d in range(n_tile):
-        for r in range(CAP):
-            cell = jnp.zeros((3, LANE), jnp.int32)
-            step = jnp.zeros((1, LANE), jnp.int32)
-            for b in range(n_blk):
-                hit = jnp.where((target[b] == d) & (rank[b] == r), 1, 0)
-                cell = cell + seeds_ref[b] * hit
-                step = step + steps_ref[b : b + 1] * hit
-            seed_out[d, 4 * r : 4 * r + 3] = cell
-            seed_out[d, 4 * r + 3 : 4 * r + 4] = step
+    own_vel = ext.at[0:3, 2 : X + 2, 0:Y, 0:Z]
+    own_visc = ext.at[3, 2 : X + 2, 0:Y, 0:Z]
+    loads = [
+        pltpu.make_async_copy(src, dst, load_sem.at[i])
+        for i, (src, dst) in enumerate((
+            (vel_hbm, own_vel), (visc_hbm, own_visc), (seeds_hbm, seeds_ref),
+            (steps_hbm, steps_ref), (dest_hbm, dest_ref),
+        ))
+    ]
+    for load in loads:
+        load.start()
+    loads[0].wait()
+    loads[1].wait()
 
     lane = lax.broadcasted_iota(jnp.int32, (Y, LANE), 1)
     packed = jnp.zeros((Y, LANE), jnp.float32)
-    for c in range(4):
-        for x in range(X):
-            k = c * X + x
-            plane = vel_ref[c, x] if c < 3 else visc_ref[x]
+    for x in range(X):
+        for c in range(4):
+            k = x * 4 + c
+            plane = ext[c, x + 2, 0:Y, 0:Z]
             if Z == LANE:
                 edge = plane
             else:
@@ -91,8 +88,23 @@
 
     pl.semaphore_wait(barrier, len(peers))
 
+    def allowed(kind, dy):
+        if kind == "seed" or dy == 0:
+            return None, None
+        return (high_open, low_open) if dy == 1 else (low_open, high_open)
+
+    def guarded(condition, action):
+        if condition is None:
+            action()
+        else:
+            pl.when(condition)(action)
+
+    wide_rows = {0: (0, 8 * X), 1: (8 * X - 16, 16), -1: (0, 16)}
     copies = {}
-    for m, (kind, dx, dy, dz) in enumerate(messages):
+
+    def send(message):
+        kind, dx, dy, dz = message
+        m = messages.index(message)
         if kind == "seed":
             src, dst = seed_out.at[lax.rem(t + dy, n_tile)], seed_in.at[t]
         elif kind == "col":
@@ -104,50 +116,75 @@
             else:
                 src, dst = col_out.at[0:SUB], col_edge.at[at + (1,)]
         elif kind == "row":
-            src, dst = row_out.at[1 if dy == 1 else 0], row_in.at[0 if dy == 1 else 1, dx + 1]
+            first, size = wide_rows[dx]
+            src = row_out.at[1 if dy == 1 else 0, first : first + size]
+            dst = row_in.at[0 if dy == 1 else 1, dx + 1, first : first + size]
         elif kind == "plane":
             if dx == 1:
-                src, dst = vel_ref.at[:, X - 2 : X], ext.at[0:3, 0:2, 0:Y, 0:Z]
+                src, dst = ext.at[0:3, X : X + 2, 0:Y, 0:Z], ext.at[0:3, 0:2, 0:Y, 0:Z]
             else:
-                src, dst = vel_ref.at[:, 0:2], ext.at[0:3, X + 2 : X + 4, 0:Y, 0:Z]
+                src, dst = ext.at[0:3, 2:4, 0:Y, 0:Z], ext.at[0:3, X + 2 : X + 4, 0:Y, 0:Z]
         else:
             if dx == 1:
-                src, dst = visc_ref.at[X - 1], ext.at[3, 1, 0:Y, 0:Z]
+                src, dst = ext.at[3, X + 1, 0:Y, 0:Z], ext.at[3, 1, 0:Y, 0:Z]
             else:
-                src, dst = visc_ref.at[0], ext.at[3, X + 2, 0:Y, 0:Z]
+                src, dst = ext.at[3, 2, 0:Y, 0:Z], ext.at[3, X + 2, 0:Y, 0:Z]
         copy = pltpu.make_async_remote_copy(
             src_ref=src, dst_ref=dst, send_sem=send_sem.at[m], recv_sem=recv_sem.at[m],
             device_id=device(dx, dy, dz), device_id_type=MESH,
         )
-        copy.start()
-        copies[kind, dx, dy, dz] = copy
-
+        copies[message] = copy
+        guarded(allowed(kind, dy)[0], copy.start)
+
+    def arrive(group):
+        for message in group:
+            guarded(allowed(message[0], message[2])[1], copies[message].wait_recv)
+
+    for message in planes + cols + rows:
+        send(message)
+
+    for load in loads[2:]:
+        load.wait()
+    n_blk = seeds_ref.shape[1]
+    count = counts_ref[0, 0, 0]
+    target = [jnp.where(b < count, dest_ref[0, 0, 0, b], -1) for b in range(n_blk)]
+    rank = []
+    for b in range(n_blk):
+        r = jnp.int32(0)
+        for a in range(b):
+            r = r + jnp.where(target[a] == target[b], 1, 0)
+        rank.append(r)
+    for d in range(n_tile):
+        for r in range(CAP):
+            hits = [jnp.where((target[b] == d) & (rank[b] == r), 1, 0) for b in range(n_blk)]
+            for j in range(4):
+                line = jnp.zeros((1, LANE), jnp.int32)
+                for b in range(n_blk):
+                    source = seeds_ref[j, b : b + 1] if j < 3 else steps_ref[b : b + 1]
+                    line = line + source * hits[b]
+                seed_out[d, 4 * r + j : 4 * r + j + 1] = line
+    for message in seeds:
+        send(message)
     seed_in[t] = seed_out[t]
-    ext[0:3, 2 : X + 2, 0:Y, 0:Z] = vel_ref[...]
-    ext[3, 2 : X + 2, 0:Y, 0:Z] = visc_ref[...]
-
-    low_open = t > 0
-    high_open = t < n_tile - 1
+
     spans = {0: [(x, x + 2) for x in range(X)], 1: [(X - 2, 0), (X - 1, 1)], -1: [(0, X + 2), (1, X + 3)]}
 
-    for message in rows:
-        copies[message].wait_recv()
+    arrive(rows)
     gap = jnp.zeros((SUB - 4, Z), jnp.float32)
-    for dx in (-1, 0, 1):
-        for c in range(4):
-            for x, here in spans[dx]:
+    for dx in (0, -1, 1):
+        for x, here in spans[dx]:
+            for c in range(4):
                 if c == 3 and here in (0, X + 3):
                     continue
-                k = c * X + x
+                k = x * 4 + c
                 high = jnp.where(high_open, row_in[1, dx + 1, 2 * k : 2 * k + 2], 0.0)
                 low = jnp.where(low_open, row_in[0, dx + 1, 2 * k : 2 * k + 2], 0.0)
                 ext[c, here, Y:YE, 0:Z] = jnp.concatenate([high, gap, low], 0)
 
-    for message in cols:
-        copies[message].wait_recv()
+    arrive(cols)
     sub8 = lax.broadcasted_iota(jnp.int32, (SUB, LANE), 0)
     keep8 = ((sub8 < SUB // 2) & high_open) | ((sub8 >= SUB // 2) & low_open)
-    for dx in (-1, 0, 1):
+    for dx in (0, -1, 1):
         whole = []
         for side in range(len(sides)):
             edge = jnp.where(sub8 < SUB // 2, col_edge[side, dx + 1, 1], col_edge[side, dx + 1, 0])
@@ -158,15 +195,14 @@
             whole = jnp.where(lane_e % 4 < 2, whole[0], whole[1])
         else:
             whole = whole[0]
-        for c in range(4):
-            for x, here in spans[dx]:
+        for x, here in spans[dx]:
+            for c in range(4):
                 if c == 3 and here in (0, X + 3):
                     continue
-                k = c * X + x
+                k = x * 4 + c
                 ext[c, here, :, Z:ZE] = pltpu.roll(whole, LANE - 4 * k - 2, 1)
 
-    for message in planes:
-        copies[message].wait_recv()
+    arrive(planes)
 
     row = lax.broadcasted_iota(jnp.int32, (YE, ZE), 0)
     keep = (row < Y) | ((row < Y + SUB // 2) & high_open) | ((row >= Y + SUB // 2) & low_open)
@@ -197,6 +233,22 @@
 
     lax.fori_loop(0, X + 2, flow, 0)
 
+    arrive(seeds)
+    seed_all[...] = seed_in[...]
+    for message in messages:
+        guarded(allowed(message[0], message[2])[0], copies[message].wait_send)
+
+
+def pathlines(shifted, seed_all, new_hbm, out_hbm, dense, out_ref, new_sem, out_sem):
+    _, _, _, planes, Y, Z = shifted.shape
+    X = planes - 2
+    writes = [
+        pltpu.make_async_copy(shifted.at[1, 1, c, 1 : X + 1], new_hbm.at[c], new_sem.at[c])
+        for c in range(3)
+    ]
+    for write in writes:
+        write.start()
+
     def hat(e):
         return (jnp.maximum(-e, 0.0), 1.0 - jnp.abs(e), jnp.maximum(e, 0.0))
 
@@ -225,19 +277,15 @@
         k3 = sample([0.5 * trace_step * k for k in k2])
         k4 = sample([trace_step * k for k in k3])
         for c in range(3):
-            new_ref[c, i] = k1[c]
             dense[c, i] = trace_step / 6.0 * (k1[c] + 2.0 * k2[c] + 2.0 * k3[c] + k4[c])
         return carry
 
     lax.fori_loop(0, X, trace, 0)
 
-    for message in seeds:
-        copies[message].wait_recv()
-
     sub = lax.broadcasted_iota(jnp.int32, (SUB, LANE), 0)
-    for d in range(n_tile):
+    for d in range(seed_all.shape[0]):
         for r in range(CAP):
-            points = [jnp.broadcast_to(seed_in[d, 4 * r + j : 4 * r + j + 1], (SUB, LANE)) for j in range(4)]
+            points = [jnp.broadcast_to(seed_all[d, 4 * r + j : 4 * r + j + 1], (SUB, LANE)) for j in range(4)]
             line = points[0] * Y + points[1]
             for c in range(3):
                 found = jnp.zeros((SUB, LANE), jnp.float32)
@@ -251,10 +299,13 @@
                             if Z > LANE:
                                 hit = hit & (points[2] >= z) & (points[2] < z + LANE)
                             found = jnp.where(hit, value, found)
-                out_ref[d * CAP + r, c : c + 1] = jnp.sum(found, 0, keepdims=True)
-
-    for message in messages:
-        copies[message].wait_send()
+                slot = d * CAP + r
+                out_ref[c, slot : slot + 1] = jnp.sum(found, 0, keepdims=True)
+    write = pltpu.make_async_copy(out_ref, out_hbm, out_sem)
+    write.start()
+    for other in writes:
+        other.wait()
+    write.wait()
 
 
 def shards(sizes, velocity, viscosity, counts, destination, seeds, substeps):
@@ -264,39 +315,61 @@
     sides, cols, rows, planes, seed_msgs = plan(sizes)
     total = len(cols) + len(rows) + len(planes) + len(seed_msgs)
     vmem = pl.BlockSpec(memory_space=pltpu.VMEM)
-    smem = pl.BlockSpec(memory_space=pltpu.SMEM)
-    f32 = jnp.float32
-    row_total = -(-8 * X // SUB) * SUB
-    fresh, result = pl.pallas_call(
-        functools.partial(kernel, sizes),
+    hbm = pl.BlockSpec(memory_space=pltpu.HBM)
+    f32, i32 = jnp.float32, jnp.int32
+    row_total = 8 * X
+    shifted, seed_all = pl.pallas_call(
+        functools.partial(exchange, sizes),
         out_shape=(
-            jax.ShapeDtypeStruct((3, X, Y, Z), f32),
-            jax.ShapeDtypeStruct((n_tile * CAP, 3, n_pts), f32),
+            jax.ShapeDtypeStruct((3, 3, 3, X + 2, Y, Z), f32),
+            jax.ShapeDtypeStruct((n_tile, 4 * CAP, n_pts), i32),
         ),
-        in_specs=[smem, smem, vmem, vmem, vmem, vmem],
+        in_specs=[pl.BlockSpec(memory_space=pltpu.SMEM)] + [hbm] * 5,
         out_specs=(vmem, vmem),
         scratch_shapes=[
             pltpu.VMEM((4, X + 4, Y + SUB, Z + LANE), f32),
-            pltpu.VMEM((3, 3, 3, X + 2, Y, Z), f32),
-            pltpu.VMEM((3, X, Y, Z), f32),
+            pltpu.SMEM(destination.shape, i32),
+            pltpu.VMEM((3, n_blk, n_pts), i32),
+            pltpu.VMEM((n_blk, n_pts), i32),
             pltpu.VMEM((Y, LANE), f32),
             pltpu.VMEM((2, row_total, Z), f32),
             pltpu.VMEM((len(sides), 3, Y, LANE), f32),
             pltpu.VMEM((len(sides), 3, 2, SUB, LANE), f32),
             pltpu.VMEM((2, 3, row_total, Z), f32),
-            pltpu.VMEM((n_tile, 4 * CAP, n_pts), jnp.int32),
-            pltpu.VMEM((n_tile, 4 * CAP, n_pts), jnp.int32),
+            pltpu.VMEM((n_tile, 4 * CAP, n_pts), i32),
+            pltpu.VMEM((n_tile, 4 * CAP, n_pts), i32),
             pltpu.SemaphoreType.DMA((total,)),
             pltpu.SemaphoreType.DMA((total,)),
+            pltpu.SemaphoreType.DMA((5,)),
         ],
         compiler_params=pltpu.CompilerParams(
             collective_id=0, has_side_effects=True, vmem_limit_bytes=16 * 2**20
         ),
     )(
-        counts.reshape(1), destination.reshape(n_blk), velocity, viscosity,
-        seeds.reshape(n_blk, 3, n_pts), substeps.reshape(n_blk, n_pts),
+        counts,
+        *(pltpu.with_memory_space_constraint(value, pltpu.HBM) for value in (
+            destination, velocity, viscosity,
+            jnp.transpose(seeds.reshape(n_blk, 3, n_pts), (1, 0, 2)), substeps.reshape(n_blk, n_pts),
+        )),
     )
-    return fresh, result[None, None, None]
+    slots = n_tile * CAP
+    fresh, result = pl.pallas_call(
+        pathlines,
+        out_shape=(
+            jax.ShapeDtypeStruct((3, X, Y, Z), f32),
+            jax.ShapeDtypeStruct((3, slots, n_pts), f32),
+        ),
+        in_specs=[vmem, vmem],
+        out_specs=(hbm, hbm),
+        scratch_shapes=[
+            pltpu.VMEM((3, X, Y, Z), f32),
+            pltpu.VMEM((3, slots, n_pts), f32),
+            pltpu.SemaphoreType.DMA((3,)),
+            pltpu.SemaphoreType.DMA,
+        ],
+        compiler_params=pltpu.CompilerParams(vmem_limit_bytes=16 * 2**20),
+    )(shifted, seed_all)
+    return fresh, jnp.transpose(result, (1, 0, 2))[None, None, None]
 
 
 def solution(mesh):

time: 22 us -> 17.5 us (0.80)
  local copies, waits for them, and re-layouts: 3.59 us -> 0 us
  Pallas kernels: 16.8 us -> 16.1 us
    unnamed x13 -> x0, local copies, waits for them, and re-layouts: 3.59 us -> none
    pallas_call x1 -> x2, Pallas kernels: 16.8 us -> 16.1 us  [the longest x1 14.4 us: shards(): pl.pallas_call(functools.partial(exchange, sizes), out_shape=(jax.ShapeDt...]
where the time goes in v2:
time: 17.5 us; the launch traced here: 17.4 us
  Pallas kernels  16.1 us (92%)
  between operations  1.28 us (7%)
    pallas_call x1, Pallas kernels, shards(): pl.pallas_call(functools.partial(exchange, sizes), out_shape=(jax.ShapeDt...  14.4 us
    pallas_call x1, Pallas kernels, shards(): pl.pallas_call(pathlines, out_shape=(jax.ShapeDtypeStruct((3, X, Y, Z), f...  1.7 us

profile of v2, /device:TPU:0, one launch (start us, length us, event | category | flops | bytes accessed | tf_op | source)
XLA Modules:
  0.0 17.4 jit_solution(10432844065700034535)
XLA Ops:
  1.3 14.4 %shard_map.77 = (f32[3,3,3,6,16,128]{5,4,3,2,1,0:T(8,128)S(1)}, s32[4,8,128]{2,1,0:T(8,128)S(1)}) custom-call(s32[1,1,1]{2,1,0:T(1,128)S(6)} %copy.8.counts_ref, s32[1,1,1,4]{3,2,1,0:T(1,128)} %dest_hbm.1, f32[3,4,16,128]{3,2,1,0:T(8,128)} %vel_hbm.1, f32[4,16,128]{2,1,0:T(8,128)} %visc_hbm.1, s32[3,4,128]{2,1,0:T(4,128)} %bitcast.7, s32[4,128]{1,0:T(4,128)} %bitcast.8), custom_call_target="tpu_custom_call" | custom-call | tf_op jit(solution)/shard_map/pallas_call | solution.py:321
  15.7 1.7 %shard_map.78 = (f32[3,4,16,128]{3,2,1,0:T(8,128)}, f32[3,8,128]{2,1,0:T(8,128)}) custom-call(f32[3,3,3,6,16,128]{5,4,3,2,1,0:T(8,128)S(1)} %get-tuple-element.6.shifted, s32[4,8,128]{2,1,0:T(8,128)S(1)} %get-tuple-element.7.seed_all), custom_call_target="tpu_custom_call" | custom-call | tf_op jit(solution)/shard_map/pallas_call | solution.py:356

commit v3 on v2

--- a/solution.py
+++ b/solution.py
@@ -20,11 +20,12 @@
 def plan(sizes):
     n_wide, n_sec, n_tile = sizes
     sides = (1,) if n_sec == 2 else (1, -1)
-    rows = [("row", dx, dy, 0) for dx in (-1, 0, 1) for dy in (-1, 1)]
-    cols = [("col", dx, dy, dz) for dz in sides for dx in (-1, 0, 1) for dy in (-1, 0, 1)]
+    rows = [("row", 0, dy, 0) for dy in (-1, 1)]
+    cols = [("col", 0, dy, dz) for dz in sides for dy in (-1, 1, 0)]
     planes = [("plane", dx, 0, 0) for dx in (-1, 1)] + [("visc", dx, 0, 0) for dx in (-1, 1)]
+    passed = [(kind, dx, 0, 0) for kind in ("passed cols", "passed rows") for dx in (-1, 1)]
     seeds = [("seed", 0, dy, 0) for dy in range(1, n_tile)]
-    return sides, cols, rows, planes, seeds
+    return sides, cols, rows, planes, passed, seeds
 
 
 def exchange(
@@ -32,15 +33,15 @@
     counts_ref, dest_hbm, vel_hbm, visc_hbm, seeds_hbm, steps_hbm,
     shifted, seed_all,
     ext, dest_ref, seeds_ref, steps_ref,
-    col_out, row_out, col_mid, col_edge, row_in, seed_out, seed_in,
+    col_out, row_out, col_in, row_in, seed_out, seed_in,
     send_sem, recv_sem, load_sem,
 ):
     n_wide, n_sec, n_tile = sizes
     _, X, Y, Z = vel_hbm.shape
     YE, ZE = Y + SUB, Z + LANE
     w, s, t = lax.axis_index("wide"), lax.axis_index("sec"), lax.axis_index("tile")
-    sides, cols, rows, planes, seeds = plan(sizes)
-    messages = planes + cols + rows + seeds
+    sides, cols, rows, planes, passed, seeds = plan(sizes)
+    messages = planes + cols + rows + passed + seeds
     low_open = t > 0
     high_open = t < n_tile - 1
 
@@ -67,6 +68,65 @@
     ]
     for load in loads:
         load.start()
+    pl.semaphore_wait(barrier, len(peers))
+
+    def allowed(kind, dy):
+        if kind == "seed" or dy == 0:
+            return None, None
+        return (high_open, low_open) if dy == 1 else (low_open, high_open)
+
+    def guarded(condition, action):
+        if condition is None:
+            action()
+        else:
+            pl.when(condition)(action)
+
+    copies = {}
+
+    def send(message):
+        kind, dx, dy, dz = message
+        m = messages.index(message)
+        if kind == "seed":
+            src, dst = seed_out.at[lax.rem(t + dy, n_tile)], seed_in.at[t]
+        elif kind == "col":
+            side = sides.index(dz)
+            if dy == 0:
+                src, dst = col_out, col_in.at[side, 1, 0:Y]
+            elif dy == 1:
+                src, dst = col_out.at[Y - SUB : Y], col_in.at[side, 1, Y : Y + SUB]
+            else:
+                src, dst = col_out.at[0:SUB], col_in.at[side, 1, Y + SUB : Y + 2 * SUB]
+        elif kind == "row":
+            src, dst = (row_out.at[1], row_in.at[1, :, 0]) if dy == 1 else (row_out.at[0], row_in.at[1, :, 1])
+        elif kind == "passed cols":
+            src, dst = col_in.at[:, 1], col_in.at[:, dx + 1]
+        elif kind == "passed rows":
+            first = X - 2 if dx == 1 else 0
+            src, dst = row_in.at[1, first : first + 2], row_in.at[dx + 1, first : first + 2]
+        elif kind == "plane":
+            if dx == 1:
+                src, dst = vel_hbm.at[:, X - 2 : X], ext.at[0:3, 0:2, 0:Y, 0:Z]
+            else:
+                src, dst = vel_hbm.at[:, 0:2], ext.at[0:3, X + 2 : X + 4, 0:Y, 0:Z]
+        else:
+            if dx == 1:
+                src, dst = visc_hbm.at[X - 1], ext.at[3, 1, 0:Y, 0:Z]
+            else:
+                src, dst = visc_hbm.at[0], ext.at[3, X + 2, 0:Y, 0:Z]
+        copy = pltpu.make_async_remote_copy(
+            src_ref=src, dst_ref=dst, send_sem=send_sem.at[m], recv_sem=recv_sem.at[m],
+            device_id=device(dx, dy, dz), device_id_type=MESH,
+        )
+        copies[message] = copy
+        guarded(allowed(kind, dy)[0], copy.start)
+
+    def arrive(group):
+        for message in group:
+            guarded(allowed(message[0], message[2])[1], copies[message].wait_recv)
+
+    for message in planes:
+        send(message)
+
     loads[0].wait()
     loads[1].wait()
 
@@ -82,65 +142,10 @@
                 edge = jnp.where(lane < LANE // 2, plane[:, :LANE], plane[:, Z - LANE :])
             moved = pltpu.roll(edge, (4 * k + 2) % LANE, 1)
             packed = jnp.where((lane >= 4 * k) & (lane < 4 * k + 4), moved, packed)
-            row_out[0, 2 * k : 2 * k + 2] = plane[0:2]
-            row_out[1, 2 * k : 2 * k + 2] = plane[Y - 2 : Y]
+            row_out[0, x, 2 * c : 2 * c + 2] = plane[0:2]
+            row_out[1, x, 2 * c : 2 * c + 2] = plane[Y - 2 : Y]
     col_out[...] = packed
-
-    pl.semaphore_wait(barrier, len(peers))
-
-    def allowed(kind, dy):
-        if kind == "seed" or dy == 0:
-            return None, None
-        return (high_open, low_open) if dy == 1 else (low_open, high_open)
-
-    def guarded(condition, action):
-        if condition is None:
-            action()
-        else:
-            pl.when(condition)(action)
-
-    wide_rows = {0: (0, 8 * X), 1: (8 * X - 16, 16), -1: (0, 16)}
-    copies = {}
-
-    def send(message):
-        kind, dx, dy, dz = message
-        m = messages.index(message)
-        if kind == "seed":
-            src, dst = seed_out.at[lax.rem(t + dy, n_tile)], seed_in.at[t]
-        elif kind == "col":
-            at = (sides.index(dz), dx + 1)
-            if dy == 0:
-                src, dst = col_out, col_mid.at[at]
-            elif dy == 1:
-                src, dst = col_out.at[Y - SUB : Y], col_edge.at[at + (0,)]
-            else:
-                src, dst = col_out.at[0:SUB], col_edge.at[at + (1,)]
-        elif kind == "row":
-            first, size = wide_rows[dx]
-            src = row_out.at[1 if dy == 1 else 0, first : first + size]
-            dst = row_in.at[0 if dy == 1 else 1, dx + 1, first : first + size]
-        elif kind == "plane":
-            if dx == 1:
-                src, dst = ext.at[0:3, X : X + 2, 0:Y, 0:Z], ext.at[0:3, 0:2, 0:Y, 0:Z]
-            else:
-                src, dst = ext.at[0:3, 2:4, 0:Y, 0:Z], ext.at[0:3, X + 2 : X + 4, 0:Y, 0:Z]
-        else:
-            if dx == 1:
-                src, dst = ext.at[3, X + 1, 0:Y, 0:Z], ext.at[3, 1, 0:Y, 0:Z]
-            else:
-                src, dst = ext.at[3, 2, 0:Y, 0:Z], ext.at[3, X + 2, 0:Y, 0:Z]
-        copy = pltpu.make_async_remote_copy(
-            src_ref=src, dst_ref=dst, send_sem=send_sem.at[m], recv_sem=recv_sem.at[m],
-            device_id=device(dx, dy, dz), device_id_type=MESH,
-        )
-        copies[message] = copy
-        guarded(allowed(kind, dy)[0], copy.start)
-
-    def arrive(group):
-        for message in group:
-            guarded(allowed(message[0], message[2])[1], copies[message].wait_recv)
-
-    for message in planes + cols + rows:
+    for message in cols + rows:
         send(message)
 
     for load in loads[2:]:
@@ -167,42 +172,36 @@
         send(message)
     seed_in[t] = seed_out[t]
 
+    arrive(cols)
+    for message in passed[0:2]:
+        send(message)
+    arrive(rows)
+    for message in passed[2:4]:
+        send(message)
+
     spans = {0: [(x, x + 2) for x in range(X)], 1: [(X - 2, 0), (X - 1, 1)], -1: [(0, X + 2), (1, X + 3)]}
-
-    arrive(rows)
     gap = jnp.zeros((SUB - 4, Z), jnp.float32)
-    for dx in (0, -1, 1):
+    sub8 = lax.broadcasted_iota(jnp.int32, (SUB, LANE), 0)
+    keep8 = ((sub8 < SUB // 2) & high_open) | ((sub8 >= SUB // 2) & low_open)
+    lane_e = lax.broadcasted_iota(jnp.int32, (YE, LANE), 1)
+
+    def unpack(dx):
+        whole = []
+        for side in range(len(sides)):
+            low, high = (col_in[side, dx + 1, Y + n : Y + n + SUB] for n in (0, SUB))
+            edge = jnp.where(keep8, jnp.where(sub8 < SUB // 2, high, low), 0.0)
+            whole.append(jnp.concatenate([col_in[side, dx + 1, 0:Y], edge], 0))
+        whole = whole[0] if len(sides) == 1 else jnp.where(lane_e % 4 < 2, whole[0], whole[1])
         for x, here in spans[dx]:
             for c in range(4):
                 if c == 3 and here in (0, X + 3):
                     continue
-                k = x * 4 + c
-                high = jnp.where(high_open, row_in[1, dx + 1, 2 * k : 2 * k + 2], 0.0)
-                low = jnp.where(low_open, row_in[0, dx + 1, 2 * k : 2 * k + 2], 0.0)
+                high = jnp.where(high_open, row_in[dx + 1, x, 1, 2 * c : 2 * c + 2], 0.0)
+                low = jnp.where(low_open, row_in[dx + 1, x, 0, 2 * c : 2 * c + 2], 0.0)
                 ext[c, here, Y:YE, 0:Z] = jnp.concatenate([high, gap, low], 0)
-
-    arrive(cols)
-    sub8 = lax.broadcasted_iota(jnp.int32, (SUB, LANE), 0)
-    keep8 = ((sub8 < SUB // 2) & high_open) | ((sub8 >= SUB // 2) & low_open)
-    for dx in (0, -1, 1):
-        whole = []
-        for side in range(len(sides)):
-            edge = jnp.where(sub8 < SUB // 2, col_edge[side, dx + 1, 1], col_edge[side, dx + 1, 0])
-            edge = jnp.where(keep8, edge, 0.0)
-            whole.append(jnp.concatenate([col_mid[side, dx + 1], edge], 0))
-        if len(sides) == 2:
-            lane_e = lax.broadcasted_iota(jnp.int32, (YE, LANE), 1)
-            whole = jnp.where(lane_e % 4 < 2, whole[0], whole[1])
-        else:
-            whole = whole[0]
-        for x, here in spans[dx]:
-            for c in range(4):
-                if c == 3 and here in (0, X + 3):
-                    continue
-                k = x * 4 + c
-                ext[c, here, :, Z:ZE] = pltpu.roll(whole, LANE - 4 * k - 2, 1)
-
-    arrive(planes)
+                ext[c, here, :, Z:ZE] = pltpu.roll(whole, LANE - 4 * (x * 4 + c) - 2, 1)
+
+    unpack(0)
 
     row = lax.broadcasted_iota(jnp.int32, (YE, ZE), 0)
     keep = (row < Y) | ((row < Y + SUB // 2) & high_open) | ((row >= Y + SUB // 2) & low_open)
@@ -231,7 +230,11 @@
                     shifted[dy, dz, c, i] = moved[0:Y]
         return carry
 
-    lax.fori_loop(0, X + 2, flow, 0)
+    lax.fori_loop(2, X, flow, 0)
+    arrive(planes + passed)
+    unpack(1)
+    unpack(-1)
+    lax.fori_loop(0, 4, lambda n, carry: flow(n + (n // 2) * (X - 2), carry), 0)
 
     arrive(seeds)
     seed_all[...] = seed_in[...]
@@ -312,12 +315,11 @@
     _, X, Y, Z = velocity.shape
     n_wide, n_sec, n_tile = sizes
     n_blk, _, n_pts = seeds.shape[3:]
-    sides, cols, rows, planes, seed_msgs = plan(sizes)
-    total = len(cols) + len(rows) + len(planes) + len(seed_msgs)
+    sides, cols, rows, planes, passed, seed_msgs = plan(sizes)
+    total = len(cols) + len(rows) + len(planes) + len(passed) + len(seed_msgs)
     vmem = pl.BlockSpec(memory_space=pltpu.VMEM)
     hbm = pl.BlockSpec(memory_space=pltpu.HBM)
     f32, i32 = jnp.float32, jnp.int32
-    row_total = 8 * X
     shifted, seed_all = pl.pallas_call(
         functools.partial(exchange, sizes),
         out_shape=(
@@ -332,10 +334,9 @@
             pltpu.VMEM((3, n_blk, n_pts), i32),
             pltpu.VMEM((n_blk, n_pts), i32),
             pltpu.VMEM((Y, LANE), f32),
-            pltpu.VMEM((2, row_total, Z), f32),
-            pltpu.VMEM((len(sides), 3, Y, LANE), f32),
-            pltpu.VMEM((len(sides), 3, 2, SUB, LANE), f32),
-            pltpu.VMEM((2, 3, row_total, Z), f32),
+            pltpu.VMEM((2, X, SUB, Z), f32),
+            pltpu.VMEM((len(sides), 3, Y + 2 * SUB, LANE), f32),
+            pltpu.VMEM((3, X, 2, SUB, Z), f32),
             pltpu.VMEM((n_tile, 4 * CAP, n_pts), i32),
             pltpu.VMEM((n_tile, 4 * CAP, n_pts), i32),
             pltpu.SemaphoreType.DMA((total,)),

time: 17.5 us -> 17.3 us (0.989)
  Pallas kernels: 16.1 us -> 15.9 us
    pallas_call x1, Pallas kernels: 14.4 us -> 14.2 us  [shards(): pl.pallas_call(functools.partial(exchange, sizes), out_shape=(jax.ShapeDt...]
where the time goes in v3:
time: 17.3 us; the launch traced here: 17.1 us
  Pallas kernels  15.9 us (92%)
  between operations  1.28 us (7%)
    pallas_call x1, Pallas kernels, shards(): pl.pallas_call(functools.partial(exchange, sizes), out_shape=(jax.ShapeDt...  14.2 us
    pallas_call x1, Pallas kernels, shards(): pl.pallas_call(pathlines, out_shape=(jax.ShapeDtypeStruct((3, X, Y, Z), f...  1.7 us

profile of v3, /device:TPU:0, one launch (start us, length us, event | category | flops | bytes accessed | tf_op | source)
XLA Modules:
  0.0 17.1 jit_solution(1165843429758636690)
XLA Ops:
  1.3 14.2 %shard_map.77 = (f32[3,3,3,6,16,128]{5,4,3,2,1,0:T(8,128)S(1)}, s32[4,8,128]{2,1,0:T(8,128)S(1)}) custom-call(s32[1,1,1]{2,1,0:T(1,128)S(6)} %copy.8.counts_ref, s32[1,1,1,4]{3,2,1,0:T(1,128)} %dest_hbm.1, f32[3,4,16,128]{3,2,1,0:T(8,128)} %vel_hbm.1, f32[4,16,128]{2,1,0:T(8,128)} %visc_hbm.1, s32[3,4,128]{2,1,0:T(4,128)} %bitcast.7, s32[4,128]{1,0:T(4,128)} %bitcast.8), custom_call_target="tpu_custom_call" | custom-call | tf_op jit(solution)/shard_map/pallas_call | solution.py:323
  15.4 1.7 %shard_map.78 = (f32[3,4,16,128]{3,2,1,0:T(8,128)}, f32[3,8,128]{2,1,0:T(8,128)}) custom-call(f32[3,3,3,6,16,128]{5,4,3,2,1,0:T(8,128)S(1)} %get-tuple-element.6.shifted, s32[4,8,128]{2,1,0:T(8,128)S(1)} %get-tuple-element.7.seed_all), custom_call_target="tpu_custom_call" | custom-call | tf_op jit(solution)/shard_map/pallas_call | solution.py:357

commit v4 on v3

--- a/solution.py
+++ b/solution.py
@@ -33,7 +33,7 @@
     counts_ref, dest_hbm, vel_hbm, visc_hbm, seeds_hbm, steps_hbm,
     shifted, seed_all,
     ext, dest_ref, seeds_ref, steps_ref,
-    col_out, row_out, col_in, row_in, seed_out, seed_in,
+    col_out, row_out, col_in, row_in, pass_col_out, pass_col_in, pass_row_out, pass_row_in, seed_out, seed_in,
     send_sem, recv_sem, load_sem,
 ):
     n_wide, n_sec, n_tile = sizes
@@ -51,11 +51,6 @@
             lax.rem(s + (dz + n_sec), n_sec),
             lax.rem(t + (dy + n_tile), n_tile),
         )
-
-    peers = sorted({(dx % n_wide, dy % n_tile, dz % n_sec) for _, dx, dy, dz in messages})
-    barrier = pltpu.get_barrier_semaphore()
-    for peer in peers:
-        pl.semaphore_signal(barrier, inc=1, device_id=device(*peer), device_id_type=MESH)
 
     own_vel = ext.at[0:3, 2 : X + 2, 0:Y, 0:Z]
     own_visc = ext.at[3, 2 : X + 2, 0:Y, 0:Z]
@@ -68,6 +63,12 @@
     ]
     for load in loads:
         load.start()
+
+    peers = sorted({(dx % n_wide, dy % n_tile, dz % n_sec) for _, dx, dy, dz in messages})
+    barrier = pltpu.get_barrier_semaphore()
+    for peer in peers:
+        pl.semaphore_signal(barrier, inc=1, device_id=device(*peer), device_id_type=MESH)
+
     pl.semaphore_wait(barrier, len(peers))
 
     def allowed(kind, dy):
@@ -91,18 +92,17 @@
         elif kind == "col":
             side = sides.index(dz)
             if dy == 0:
-                src, dst = col_out, col_in.at[side, 1, 0:Y]
+                src, dst = col_out, col_in.at[side, 0:Y]
             elif dy == 1:
-                src, dst = col_out.at[Y - SUB : Y], col_in.at[side, 1, Y : Y + SUB]
+                src, dst = col_out.at[Y - SUB : Y], col_in.at[side, Y : Y + SUB]
             else:
-                src, dst = col_out.at[0:SUB], col_in.at[side, 1, Y + SUB : Y + 2 * SUB]
+                src, dst = col_out.at[0:SUB], col_in.at[side, Y + SUB : Y + 2 * SUB]
         elif kind == "row":
-            src, dst = (row_out.at[1], row_in.at[1, :, 0]) if dy == 1 else (row_out.at[0], row_in.at[1, :, 1])
+            src, dst = (row_out.at[1], row_in.at[:, 0]) if dy == 1 else (row_out.at[0], row_in.at[:, 1])
         elif kind == "passed cols":
-            src, dst = col_in.at[:, 1], col_in.at[:, dx + 1]
+            src, dst = pass_col_out.at[(dx + 1) // 2], pass_col_in.at[(dx + 1) // 2]
         elif kind == "passed rows":
-            first = X - 2 if dx == 1 else 0
-            src, dst = row_in.at[1, first : first + 2], row_in.at[dx + 1, first : first + 2]
+            src, dst = pass_row_out.at[(dx + 1) // 2], pass_row_in.at[(dx + 1) // 2]
         elif kind == "plane":
             if dx == 1:
                 src, dst = vel_hbm.at[:, X - 2 : X], ext.at[0:3, 0:2, 0:Y, 0:Z]
@@ -172,32 +172,69 @@
         send(message)
     seed_in[t] = seed_out[t]
 
+    sub8 = lax.broadcasted_iota(jnp.int32, (SUB, LANE), 0)
+    lane8 = lax.broadcasted_iota(jnp.int32, (SUB, LANE), 1)
+    groups = Y // SUB + 2
+    wide_lanes = 32
+    per_tile = LANE // wide_lanes
+    first_lane = {-1: 0, 1: 16 * (X - 2)}
+
     arrive(cols)
     for message in passed[0:2]:
+        dx = message[1]
+        for side in range(len(sides)):
+            for tile in range(-(-groups // per_tile)):
+                held = jnp.zeros((SUB, LANE), jnp.float32)
+                for q in range(min(per_tile, groups - tile * per_tile)):
+                    at = (tile * per_tile + q) * SUB
+                    group = pltpu.roll(col_in[side, at : at + SUB], (wide_lanes * q - first_lane[dx]) % LANE, 1)
+                    held = jnp.where((lane8 >= wide_lanes * q) & (lane8 < wide_lanes * (q + 1)), group, held)
+                pass_col_out[(dx + 1) // 2, side, tile] = held
         send(message)
     arrive(rows)
     for message in passed[2:4]:
+        dx = message[1]
+        near, far = (X - 1, X - 2) if dx == 1 else (0, 1)
+        n = (dx + 1) // 2
+        pass_row_out[n, 0:2] = row_in[near]
+        for c in range(4):
+            pass_row_out[n, 2, c : c + 1] = row_in[far, 0, 2 * c + 1 : 2 * c + 2]
+            pass_row_out[n, 2, 4 + c : 5 + c] = row_in[far, 1, 2 * c : 2 * c + 1]
         send(message)
 
     spans = {0: [(x, x + 2) for x in range(X)], 1: [(X - 2, 0), (X - 1, 1)], -1: [(0, X + 2), (1, X + 3)]}
-    gap = jnp.zeros((SUB - 4, Z), jnp.float32)
-    sub8 = lax.broadcasted_iota(jnp.int32, (SUB, LANE), 0)
     keep8 = ((sub8 < SUB // 2) & high_open) | ((sub8 >= SUB // 2) & low_open)
     lane_e = lax.broadcasted_iota(jnp.int32, (YE, LANE), 1)
 
     def unpack(dx):
+        n = (dx + 1) // 2
         whole = []
         for side in range(len(sides)):
-            low, high = (col_in[side, dx + 1, Y + n : Y + n + SUB] for n in (0, SUB))
-            edge = jnp.where(keep8, jnp.where(sub8 < SUB // 2, high, low), 0.0)
-            whole.append(jnp.concatenate([col_in[side, dx + 1, 0:Y], edge], 0))
+            if dx == 0:
+                parts = [col_in[side, g * SUB : (g + 1) * SUB] for g in range(groups)]
+            else:
+                parts = [
+                    pltpu.roll(
+                        pass_col_in[n, side, g // per_tile],
+                        (first_lane[dx] - wide_lanes * (g % per_tile)) % LANE, 1,
+                    )
+                    for g in range(groups)
+                ]
+            edge = jnp.where(keep8, jnp.where(sub8 < SUB // 2, parts[-1], parts[-2]), 0.0)
+            whole.append(jnp.concatenate(parts[:-2] + [edge], 0))
         whole = whole[0] if len(sides) == 1 else jnp.where(lane_e % 4 < 2, whole[0], whole[1])
         for x, here in spans[dx]:
-            for c in range(4):
-                if c == 3 and here in (0, X + 3):
-                    continue
-                high = jnp.where(high_open, row_in[dx + 1, x, 1, 2 * c : 2 * c + 2], 0.0)
-                low = jnp.where(low_open, row_in[dx + 1, x, 0, 2 * c : 2 * c + 2], 0.0)
+            far = here in (0, X + 3)
+            for c in range(3 if far else 4):
+                if far:
+                    high, low = pass_row_in[n, 2, 4 + c : 5 + c], pass_row_in[n, 2, c : c + 1]
+                elif dx == 0:
+                    high, low = row_in[x, 1, 2 * c : 2 * c + 2], row_in[x, 0, 2 * c : 2 * c + 2]
+                else:
+                    high, low = pass_row_in[n, 1, 2 * c : 2 * c + 2], pass_row_in[n, 0, 2 * c : 2 * c + 2]
+                high = jnp.where(high_open, high, 0.0)
+                low = jnp.where(low_open, low, 0.0)
+                gap = jnp.zeros((SUB - 2 * high.shape[0], Z), jnp.float32)
                 ext[c, here, Y:YE, 0:Z] = jnp.concatenate([high, gap, low], 0)
                 ext[c, here, :, Z:ZE] = pltpu.roll(whole, LANE - 4 * (x * 4 + c) - 2, 1)
 
@@ -335,8 +372,12 @@
             pltpu.VMEM((n_blk, n_pts), i32),
             pltpu.VMEM((Y, LANE), f32),
             pltpu.VMEM((2, X, SUB, Z), f32),
-            pltpu.VMEM((len(sides), 3, Y + 2 * SUB, LANE), f32),
-            pltpu.VMEM((3, X, 2, SUB, Z), f32),
+            pltpu.VMEM((len(sides), Y + 2 * SUB, LANE), f32),
+            pltpu.VMEM((X, 2, SUB, Z), f32),
+            pltpu.VMEM((2, len(sides), -(-(Y // SUB + 2) // 4), SUB, LANE), f32),
+            pltpu.VMEM((2, len(sides), -(-(Y // SUB + 2) // 4), SUB, LANE), f32),
+            pltpu.VMEM((2, 3, SUB, Z), f32),
+            pltpu.VMEM((2, 3, SUB, Z), f32),
             pltpu.VMEM((n_tile, 4 * CAP, n_pts), i32),
             pltpu.VMEM((n_tile, 4 * CAP, n_pts), i32),
             pltpu.SemaphoreType.DMA((total,)),

time: 17.3 us -> 16.6 us (0.960)
  Pallas kernels: 15.9 us -> 15.2 us
    pallas_call x1, Pallas kernels: 14.2 us -> 13.5 us  [shards(): pl.pallas_call(functools.partial(exchange, sizes), out_shape=(jax.ShapeDt...]
where the time goes in v4:
time: 16.6 us; the launch traced here: 16.5 us
  Pallas kernels  15.2 us (92%)
  between operations  1.28 us (8%)
    pallas_call x1, Pallas kernels, shards(): pl.pallas_call(functools.partial(exchange, sizes), out_shape=(jax.ShapeDt...  13.5 us
    pallas_call x1, Pallas kernels, shards(): pl.pallas_call(pathlines, out_shape=(jax.ShapeDtypeStruct((3, X, Y, Z), f...  1.7 us

profile of v4, /device:TPU:0, one launch (start us, length us, event | category | flops | bytes accessed | tf_op | source)
XLA Modules:
  0.0 16.5 jit_solution(5412835157121135249)
XLA Ops:
  1.3 13.5 %shard_map.77 = (f32[3,3,3,6,16,128]{5,4,3,2,1,0:T(8,128)S(1)}, s32[4,8,128]{2,1,0:T(8,128)S(1)}) custom-call(s32[1,1,1]{2,1,0:T(1,128)S(6)} %copy.8.counts_ref, s32[1,1,1,4]{3,2,1,0:T(1,128)} %dest_hbm.1, f32[3,4,16,128]{3,2,1,0:T(8,128)} %vel_hbm.1, f32[4,16,128]{2,1,0:T(8,128)} %visc_hbm.1, s32[3,4,128]{2,1,0:T(4,128)} %bitcast.7, s32[4,128]{1,0:T(4,128)} %bitcast.8), custom_call_target="tpu_custom_call" | custom-call | tf_op jit(solution)/shard_map/pallas_call | solution.py:360
  14.8 1.7 %shard_map.78 = (f32[3,4,16,128]{3,2,1,0:T(8,128)}, f32[3,8,128]{2,1,0:T(8,128)}) custom-call(f32[3,3,3,6,16,128]{5,4,3,2,1,0:T(8,128)S(1)} %get-tuple-element.6.shifted, s32[4,8,128]{2,1,0:T(8,128)S(1)} %get-tuple-element.7.seed_all), custom_call_target="tpu_custom_call" | custom-call | tf_op jit(solution)/shard_map/pallas_call | solution.py:398

commit v5 on v3

--- a/solution.py
+++ b/solution.py
@@ -22,10 +22,11 @@
     sides = (1,) if n_sec == 2 else (1, -1)
     rows = [("row", 0, dy, 0) for dy in (-1, 1)]
     cols = [("col", 0, dy, dz) for dz in sides for dy in (-1, 1, 0)]
+    diagonal = [("col", dx, dy, dz) for dz in sides for dx in (-1, 1) for dy in (-1, 1, 0)]
+    diagonal += [("row", dx, dy, 0) for dx in (-1, 1) for dy in (-1, 1)]
     planes = [("plane", dx, 0, 0) for dx in (-1, 1)] + [("visc", dx, 0, 0) for dx in (-1, 1)]
-    passed = [(kind, dx, 0, 0) for kind in ("passed cols", "passed rows") for dx in (-1, 1)]
     seeds = [("seed", 0, dy, 0) for dy in range(1, n_tile)]
-    return sides, cols, rows, planes, passed, seeds
+    return sides, cols, rows, planes, diagonal, seeds
 
 
 def exchange(
@@ -33,15 +34,15 @@
     counts_ref, dest_hbm, vel_hbm, visc_hbm, seeds_hbm, steps_hbm,
     shifted, seed_all,
     ext, dest_ref, seeds_ref, steps_ref,
-    col_out, row_out, col_in, row_in, seed_out, seed_in,
+    mid_out, edge_out, row_out, mid_in, edge_in, row_in, seed_out, seed_in,
     send_sem, recv_sem, load_sem,
 ):
     n_wide, n_sec, n_tile = sizes
     _, X, Y, Z = vel_hbm.shape
     YE, ZE = Y + SUB, Z + LANE
     w, s, t = lax.axis_index("wide"), lax.axis_index("sec"), lax.axis_index("tile")
-    sides, cols, rows, planes, passed, seeds = plan(sizes)
-    messages = planes + cols + rows + passed + seeds
+    sides, cols, rows, planes, diagonal, seeds = plan(sizes)
+    messages = planes + diagonal + cols + rows + seeds
     low_open = t > 0
     high_open = t < n_tile - 1
 
@@ -51,11 +52,6 @@
             lax.rem(s + (dz + n_sec), n_sec),
             lax.rem(t + (dy + n_tile), n_tile),
         )
-
-    peers = sorted({(dx % n_wide, dy % n_tile, dz % n_sec) for _, dx, dy, dz in messages})
-    barrier = pltpu.get_barrier_semaphore()
-    for peer in peers:
-        pl.semaphore_signal(barrier, inc=1, device_id=device(*peer), device_id_type=MESH)
 
     own_vel = ext.at[0:3, 2 : X + 2, 0:Y, 0:Z]
     own_visc = ext.at[3, 2 : X + 2, 0:Y, 0:Z]
@@ -68,6 +64,12 @@
     ]
     for load in loads:
         load.start()
+
+    peers = sorted({(dx % n_wide, dy % n_tile, dz % n_sec) for _, dx, dy, dz in messages})
+    barrier = pltpu.get_barrier_semaphore()
+    for peer in peers:
+        pl.semaphore_signal(barrier, inc=1, device_id=device(*peer), device_id_type=MESH)
+
     pl.semaphore_wait(barrier, len(peers))
 
     def allowed(kind, dy):
@@ -89,20 +91,15 @@
         if kind == "seed":
             src, dst = seed_out.at[lax.rem(t + dy, n_tile)], seed_in.at[t]
         elif kind == "col":
-            side = sides.index(dz)
+            at = (sides.index(dz), dx + 1)
             if dy == 0:
-                src, dst = col_out, col_in.at[side, 1, 0:Y]
-            elif dy == 1:
-                src, dst = col_out.at[Y - SUB : Y], col_in.at[side, 1, Y : Y + SUB]
+                src, dst = mid_out, mid_in.at[at]
             else:
-                src, dst = col_out.at[0:SUB], col_in.at[side, 1, Y + SUB : Y + 2 * SUB]
+                src, dst = (edge_out.at[1], edge_in.at[at + (0,)]) if dy == 1 else (edge_out.at[0], edge_in.at[at + (1,)])
         elif kind == "row":
-            src, dst = (row_out.at[1], row_in.at[1, :, 0]) if dy == 1 else (row_out.at[0], row_in.at[1, :, 1])
-        elif kind == "passed cols":
-            src, dst = col_in.at[:, 1], col_in.at[:, dx + 1]
-        elif kind == "passed rows":
-            first = X - 2 if dx == 1 else 0
-            src, dst = row_in.at[1, first : first + 2], row_in.at[dx + 1, first : first + 2]
+            span = {0: slice(0, X), 1: slice(X - 2, X), -1: slice(0, 2)}[dx]
+            src = row_out.at[1 if dy == 1 else 0, span]
+            dst = row_in.at[dx + 1, span, 0 if dy == 1 else 1]
         elif kind == "plane":
             if dx == 1:
                 src, dst = vel_hbm.at[:, X - 2 : X], ext.at[0:3, 0:2, 0:Y, 0:Z]
@@ -144,8 +141,20 @@
             packed = jnp.where((lane >= 4 * k) & (lane < 4 * k + 4), moved, packed)
             row_out[0, x, 2 * c : 2 * c + 2] = plane[0:2]
             row_out[1, x, 2 * c : 2 * c + 2] = plane[Y - 2 : Y]
-    col_out[...] = packed
-    for message in cols + rows:
+    edge_out[0] = packed[0:SUB]
+    edge_out[1] = packed[Y - SUB : Y]
+    lane8 = lax.broadcasted_iota(jnp.int32, (SUB, LANE), 1)
+    used = 16 * X
+    per_tile = LANE // used
+    groups = Y // SUB
+    for tile in range(mid_out.shape[0]):
+        held = jnp.zeros((SUB, LANE), jnp.float32)
+        for q in range(min(per_tile, groups - tile * per_tile)):
+            at = (tile * per_tile + q) * SUB
+            group = pltpu.roll(packed[at : at + SUB], used * q, 1)
+            held = jnp.where((lane8 >= used * q) & (lane8 < used * (q + 1)), group, held)
+        mid_out[tile] = held
+    for message in diagonal + cols + rows:
         send(message)
 
     for load in loads[2:]:
@@ -167,37 +176,37 @@
                 for b in range(n_blk):
                     source = seeds_ref[j, b : b + 1] if j < 3 else steps_ref[b : b + 1]
                     line = line + source * hits[b]
-                seed_out[d, 4 * r + j : 4 * r + j + 1] = line
+                seed_out[d, CAP * j + r : CAP * j + r + 1] = line
     for message in seeds:
         send(message)
     seed_in[t] = seed_out[t]
 
     arrive(cols)
-    for message in passed[0:2]:
-        send(message)
     arrive(rows)
-    for message in passed[2:4]:
-        send(message)
+    sub8 = lax.broadcasted_iota(jnp.int32, (SUB, LANE), 0)
 
     spans = {0: [(x, x + 2) for x in range(X)], 1: [(X - 2, 0), (X - 1, 1)], -1: [(0, X + 2), (1, X + 3)]}
-    gap = jnp.zeros((SUB - 4, Z), jnp.float32)
-    sub8 = lax.broadcasted_iota(jnp.int32, (SUB, LANE), 0)
     keep8 = ((sub8 < SUB // 2) & high_open) | ((sub8 >= SUB // 2) & low_open)
     lane_e = lax.broadcasted_iota(jnp.int32, (YE, LANE), 1)
 
     def unpack(dx):
         whole = []
         for side in range(len(sides)):
-            low, high = (col_in[side, dx + 1, Y + n : Y + n + SUB] for n in (0, SUB))
-            edge = jnp.where(keep8, jnp.where(sub8 < SUB // 2, high, low), 0.0)
-            whole.append(jnp.concatenate([col_in[side, dx + 1, 0:Y], edge], 0))
+            edge = jnp.where(sub8 < SUB // 2, edge_in[side, dx + 1, 1], edge_in[side, dx + 1, 0])
+            parts = [
+                pltpu.roll(mid_in[side, dx + 1, g // per_tile], (-used * (g % per_tile)) % LANE, 1)
+                for g in range(groups)
+            ]
+            whole.append(jnp.concatenate(parts + [jnp.where(keep8, edge, 0.0)], 0))
         whole = whole[0] if len(sides) == 1 else jnp.where(lane_e % 4 < 2, whole[0], whole[1])
         for x, here in spans[dx]:
-            for c in range(4):
-                if c == 3 and here in (0, X + 3):
-                    continue
-                high = jnp.where(high_open, row_in[dx + 1, x, 1, 2 * c : 2 * c + 2], 0.0)
-                low = jnp.where(low_open, row_in[dx + 1, x, 0, 2 * c : 2 * c + 2], 0.0)
+            far = here in (0, X + 3)
+            for c in range(3 if far else 4):
+                high = row_in[dx + 1, x, 1, 2 * c : 2 * c + 2]
+                low = row_in[dx + 1, x, 0, 2 * c : 2 * c + 2]
+                high = jnp.where(high_open, high, 0.0)
+                low = jnp.where(low_open, low, 0.0)
+                gap = jnp.zeros((SUB - 4, Z), jnp.float32)
                 ext[c, here, Y:YE, 0:Z] = jnp.concatenate([high, gap, low], 0)
                 ext[c, here, :, Z:ZE] = pltpu.roll(whole, LANE - 4 * (x * 4 + c) - 2, 1)
 
@@ -231,13 +240,15 @@
         return carry
 
     lax.fori_loop(2, X, flow, 0)
-    arrive(planes + passed)
+    arrive(planes + diagonal)
     unpack(1)
     unpack(-1)
     lax.fori_loop(0, 4, lambda n, carry: flow(n + (n // 2) * (X - 2), carry), 0)
 
     arrive(seeds)
-    seed_all[...] = seed_in[...]
+    for j in range(4):
+        for d in range(n_tile):
+            seed_all[j, CAP * d : CAP * (d + 1)] = seed_in[d, CAP * j : CAP * (j + 1)]
     for message in messages:
         guarded(allowed(message[0], message[2])[0], copies[message].wait_send)
 
@@ -285,25 +296,25 @@
 
     lax.fori_loop(0, X, trace, 0)
 
-    sub = lax.broadcasted_iota(jnp.int32, (SUB, LANE), 0)
-    for d in range(seed_all.shape[0]):
-        for r in range(CAP):
-            points = [jnp.broadcast_to(seed_all[d, 4 * r + j : 4 * r + j + 1], (SUB, LANE)) for j in range(4)]
-            line = points[0] * Y + points[1]
-            for c in range(3):
-                found = jnp.zeros((SUB, LANE), jnp.float32)
-                for x in range(X):
-                    for y in range(0, Y, SUB):
-                        for z in range(0, Z, LANE):
-                            value = jnp.take_along_axis(
-                                dense[c, x, y : y + SUB, z : z + LANE], points[2] & (LANE - 1), axis=1
-                            )
-                            hit = (line == x * Y + y + sub) & (points[3] > 0)
-                            if Z > LANE:
-                                hit = hit & (points[2] >= z) & (points[2] < z + LANE)
-                            found = jnp.where(hit, value, found)
-                slot = d * CAP + r
-                out_ref[c, slot : slot + 1] = jnp.sum(found, 0, keepdims=True)
+    slots = seed_all.shape[1]
+    point_x, point_y, point_z, point_steps = (seed_all[j] for j in range(4))
+    line = jnp.where(point_steps > 0, point_x * Y + point_y, -1)
+    for z in range(0, Z, LANE):
+        place = line if Z == LANE else jnp.where((point_z >= z) & (point_z < z + LANE), line, -1)
+        index = point_z if Z == LANE else point_z & (LANE - 1)
+
+        def look(x, found):
+            found = list(found)
+            for y in range(Y):
+                hit = place == x * Y + y
+                for c in range(3):
+                    source = jnp.broadcast_to(dense[c, x, y : y + 1, z : z + LANE], (slots, LANE))
+                    found[c] = jnp.where(hit, jnp.take_along_axis(source, index, axis=1), found[c])
+            return tuple(found)
+
+        start = tuple(jnp.zeros((slots, LANE), jnp.float32) if z == 0 else out_ref[c] for c in range(3))
+        for c, value in enumerate(lax.fori_loop(0, X, look, start)):
+            out_ref[c] = value
     write = pltpu.make_async_copy(out_ref, out_hbm, out_sem)
     write.start()
     for other in writes:
@@ -315,16 +326,17 @@
     _, X, Y, Z = velocity.shape
     n_wide, n_sec, n_tile = sizes
     n_blk, _, n_pts = seeds.shape[3:]
-    sides, cols, rows, planes, passed, seed_msgs = plan(sizes)
-    total = len(cols) + len(rows) + len(planes) + len(passed) + len(seed_msgs)
+    sides, cols, rows, planes, diagonal, seed_msgs = plan(sizes)
+    total = len(cols) + len(rows) + len(planes) + len(diagonal) + len(seed_msgs)
     vmem = pl.BlockSpec(memory_space=pltpu.VMEM)
     hbm = pl.BlockSpec(memory_space=pltpu.HBM)
     f32, i32 = jnp.float32, jnp.int32
+    mid_tiles = -(-(Y // SUB) // (LANE // (16 * X)))
     shifted, seed_all = pl.pallas_call(
         functools.partial(exchange, sizes),
         out_shape=(
             jax.ShapeDtypeStruct((3, 3, 3, X + 2, Y, Z), f32),
-            jax.ShapeDtypeStruct((n_tile, 4 * CAP, n_pts), i32),
+            jax.ShapeDtypeStruct((4, n_tile * CAP, n_pts), i32),
         ),
         in_specs=[pl.BlockSpec(memory_space=pltpu.SMEM)] + [hbm] * 5,
         out_specs=(vmem, vmem),
@@ -333,9 +345,11 @@
             pltpu.SMEM(destination.shape, i32),
             pltpu.VMEM((3, n_blk, n_pts), i32),
             pltpu.VMEM((n_blk, n_pts), i32),
-            pltpu.VMEM((Y, LANE), f32),
+            pltpu.VMEM((mid_tiles, SUB, LANE), f32),
+            pltpu.VMEM((2, SUB, LANE), f32),
             pltpu.VMEM((2, X, SUB, Z), f32),
-            pltpu.VMEM((len(sides), 3, Y + 2 * SUB, LANE), f32),
+            pltpu.VMEM((len(sides), 3, mid_tiles, SUB, LANE), f32),
+            pltpu.VMEM((len(sides), 3, 2, SUB, LANE), f32),
             pltpu.VMEM((3, X, 2, SUB, Z), f32),
             pltpu.VMEM((n_tile, 4 * CAP, n_pts), i32),
             pltpu.VMEM((n_tile, 4 * CAP, n_pts), i32),

time: 17.3 us -> 17.1 us (0.988)
  Pallas kernels: 15.9 us -> 15.7 us
    pallas_call x1, Pallas kernels: 14.2 us -> 13.8 us  [shards(): pl.pallas_call(functools.partial(exchange, sizes), out_shape=(jax.ShapeDt...]
    pallas_call x1, Pallas kernels: 1.7 us -> 1.88 us  [shards(): pl.pallas_call(pathlines, out_shape=(jax.ShapeDtypeStruct((3, X, Y, Z), f...]
where the time goes in v5:
time: 17.1 us; the launch traced here: 17 us
  Pallas kernels  15.7 us (92%)
  between operations  1.28 us (7%)
    pallas_call x1, Pallas kernels, shards(): pl.pallas_call(functools.partial(exchange, sizes), out_shape=(jax.ShapeDt...  13.8 us
    pallas_call x1, Pallas kernels, shards(): pl.pallas_call(pathlines, out_shape=(jax.ShapeDtypeStruct((3, X, Y, Z), f...  1.88 us

profile of v5, /device:TPU:0, one launch (start us, length us, event | category | flops | bytes accessed | tf_op | source)
XLA Modules:
  0.0 17.0 jit_solution(12258032045462369067)
XLA Ops:
  1.3 13.8 %shard_map.77 = (f32[3,3,3,6,16,128]{5,4,3,2,1,0:T(8,128)S(1)}, s32[4,8,128]{2,1,0:T(8,128)S(1)}) custom-call(s32[1,1,1]{2,1,0:T(1,128)S(6)} %copy.8.counts_ref, s32[1,1,1,4]{3,2,1,0:T(1,128)} %dest_hbm.1, f32[3,4,16,128]{3,2,1,0:T(8,128)} %vel_hbm.1, f32[4,16,128]{2,1,0:T(8,128)} %visc_hbm.1, s32[3,4,128]{2,1,0:T(4,128)} %bitcast.7, s32[4,128]{1,0:T(4,128)} %bitcast.8), custom_call_target="tpu_custom_call" | custom-call | tf_op jit(solution)/shard_map/pallas_call | solution.py:335
  15.1 1.9 %shard_map.78 = (f32[3,4,16,128]{3,2,1,0:T(8,128)}, f32[3,8,128]{2,1,0:T(8,128)}) custom-call(f32[3,3,3,6,16,128]{5,4,3,2,1,0:T(8,128)S(1)} %get-tuple-element.6.shifted, s32[4,8,128]{2,1,0:T(8,128)S(1)} %get-tuple-element.7.seed_all), custom_call_target="tpu_custom_call" | custom-call | tf_op jit(solution)/shard_map/pallas_call | solution.py:371

commit v6 on v4

--- a/solution.py
+++ b/solution.py
@@ -22,8 +22,8 @@
     sides = (1,) if n_sec == 2 else (1, -1)
     rows = [("row", 0, dy, 0) for dy in (-1, 1)]
     cols = [("col", 0, dy, dz) for dz in sides for dy in (-1, 1, 0)]
-    planes = [("plane", dx, 0, 0) for dx in (-1, 1)] + [("visc", dx, 0, 0) for dx in (-1, 1)]
-    passed = [(kind, dx, 0, 0) for kind in ("passed cols", "passed rows") for dx in (-1, 1)]
+    planes = [("plane", dx, 0, 0) for dx in (-1, 1)]
+    passed = [("passed", dx, 0, 0) for dx in (-1, 1)]
     seeds = [("seed", 0, dy, 0) for dy in range(1, n_tile)]
     return sides, cols, rows, planes, passed, seeds
 
@@ -33,7 +33,7 @@
     counts_ref, dest_hbm, vel_hbm, visc_hbm, seeds_hbm, steps_hbm,
     shifted, seed_all,
     ext, dest_ref, seeds_ref, steps_ref,
-    col_out, row_out, col_in, row_in, pass_col_out, pass_col_in, pass_row_out, pass_row_in, seed_out, seed_in,
+    col_out, row_out, col_in, row_in, pass_out, pass_in, seed_out, seed_in,
     send_sem, recv_sem, load_sem,
 ):
     n_wide, n_sec, n_tile = sizes
@@ -45,12 +45,18 @@
     low_open = t > 0
     high_open = t < n_tile - 1
 
+    def shift(position, step, size):
+        if step % size == 0:
+            return position
+        moved = position + step % size
+        return jnp.where(moved >= size, moved - size, moved)
+
+    w_of = [shift(w, step, n_wide) for step in (0, 1, -1)]
+    s_of = [shift(s, step, n_sec) for step in (0, 1, -1)]
+    t_of = [shift(t, step, n_tile) for step in range(n_tile)]
+
     def device(dx, dy, dz):
-        return (
-            lax.rem(w + (dx + n_wide), n_wide),
-            lax.rem(s + (dz + n_sec), n_sec),
-            lax.rem(t + (dy + n_tile), n_tile),
-        )
+        return (w_of[dx], s_of[dz], t_of[dy])
 
     own_vel = ext.at[0:3, 2 : X + 2, 0:Y, 0:Z]
     own_visc = ext.at[3, 2 : X + 2, 0:Y, 0:Z]
@@ -64,9 +70,11 @@
     for load in loads:
         load.start()
 
-    peers = sorted({(dx % n_wide, dy % n_tile, dz % n_sec) for _, dx, dy, dz in messages})
+    peers = {}
+    for _, dx, dy, dz in messages:
+        peers.setdefault((dx % n_wide, dy % n_tile, dz % n_sec), (dx, dy, dz))
     barrier = pltpu.get_barrier_semaphore()
-    for peer in peers:
+    for peer in peers.values():
         pl.semaphore_signal(barrier, inc=1, device_id=device(*peer), device_id_type=MESH)
 
     pl.semaphore_wait(barrier, len(peers))
@@ -88,7 +96,7 @@
         kind, dx, dy, dz = message
         m = messages.index(message)
         if kind == "seed":
-            src, dst = seed_out.at[lax.rem(t + dy, n_tile)], seed_in.at[t]
+            src, dst = seed_out.at[t_of[dy]], seed_in.at[t]
         elif kind == "col":
             side = sides.index(dz)
             if dy == 0:
@@ -99,20 +107,12 @@
                 src, dst = col_out.at[0:SUB], col_in.at[side, Y + SUB : Y + 2 * SUB]
         elif kind == "row":
             src, dst = (row_out.at[1], row_in.at[:, 0]) if dy == 1 else (row_out.at[0], row_in.at[:, 1])
-        elif kind == "passed cols":
-            src, dst = pass_col_out.at[(dx + 1) // 2], pass_col_in.at[(dx + 1) // 2]
-        elif kind == "passed rows":
-            src, dst = pass_row_out.at[(dx + 1) // 2], pass_row_in.at[(dx + 1) // 2]
-        elif kind == "plane":
-            if dx == 1:
-                src, dst = vel_hbm.at[:, X - 2 : X], ext.at[0:3, 0:2, 0:Y, 0:Z]
-            else:
-                src, dst = vel_hbm.at[:, 0:2], ext.at[0:3, X + 2 : X + 4, 0:Y, 0:Z]
+        elif kind == "passed":
+            src, dst = pass_out.at[(dx + 1) // 2], pass_in.at[(dx + 1) // 2]
+        elif dx == 1:
+            src, dst = vel_hbm.at[:, X - 2 : X], ext.at[0:3, 0:2, 0:Y, 0:Z]
         else:
-            if dx == 1:
-                src, dst = visc_hbm.at[X - 1], ext.at[3, 1, 0:Y, 0:Z]
-            else:
-                src, dst = visc_hbm.at[0], ext.at[3, X + 2, 0:Y, 0:Z]
+            src, dst = vel_hbm.at[:, 0:2], ext.at[0:3, X + 2 : X + 4, 0:Y, 0:Z]
         copy = pltpu.make_async_remote_copy(
             src_ref=src, dst_ref=dst, send_sem=send_sem.at[m], recv_sem=recv_sem.at[m],
             device_id=device(dx, dy, dz), device_id_type=MESH,
@@ -178,28 +178,42 @@
     wide_lanes = 32
     per_tile = LANE // wide_lanes
     first_lane = {-1: 0, 1: 16 * (X - 2)}
-
+    near_of = {-1: 0, 1: X - 1}
+    far_of = {-1: 1, 1: X - 2}
+    lanes_of = [slice(z, z + LANE) for z in range(0, Z, LANE)]
+    parts_z = len(lanes_of)
+    visc_at = 3 * parts_z
+    cols_at = visc_at + parts_z * (Y // SUB)
+    col_tiles = -(-groups // per_tile)
+
+    for message in passed:
+        dx = message[1]
+        n = (dx + 1) // 2
+        for z, lanes in enumerate(lanes_of):
+            for y in range(Y // SUB):
+                pass_out[n, visc_at + z * (Y // SUB) + y] = ext[3, near_of[dx] + 2, y * SUB : (y + 1) * SUB, lanes]
     arrive(cols)
-    for message in passed[0:2]:
+    for message in passed:
         dx = message[1]
         for side in range(len(sides)):
-            for tile in range(-(-groups // per_tile)):
+            for tile in range(col_tiles):
                 held = jnp.zeros((SUB, LANE), jnp.float32)
                 for q in range(min(per_tile, groups - tile * per_tile)):
                     at = (tile * per_tile + q) * SUB
                     group = pltpu.roll(col_in[side, at : at + SUB], (wide_lanes * q - first_lane[dx]) % LANE, 1)
                     held = jnp.where((lane8 >= wide_lanes * q) & (lane8 < wide_lanes * (q + 1)), group, held)
-                pass_col_out[(dx + 1) // 2, side, tile] = held
-        send(message)
+                pass_out[(dx + 1) // 2, cols_at + side * col_tiles + tile] = held
     arrive(rows)
-    for message in passed[2:4]:
+    for message in passed:
         dx = message[1]
-        near, far = (X - 1, X - 2) if dx == 1 else (0, 1)
         n = (dx + 1) // 2
-        pass_row_out[n, 0:2] = row_in[near]
-        for c in range(4):
-            pass_row_out[n, 2, c : c + 1] = row_in[far, 0, 2 * c + 1 : 2 * c + 2]
-            pass_row_out[n, 2, 4 + c : 5 + c] = row_in[far, 1, 2 * c : 2 * c + 1]
+        near, far = near_of[dx], far_of[dx]
+        for z, lanes in enumerate(lanes_of):
+            pass_out[n, 3 * z] = row_in[near, 0, :, lanes]
+            pass_out[n, 3 * z + 1] = row_in[near, 1, :, lanes]
+            for c in range(4):
+                pass_out[n, 3 * z + 2, c : c + 1] = row_in[far, 0, 2 * c + 1 : 2 * c + 2, lanes]
+                pass_out[n, 3 * z + 2, 4 + c : 5 + c] = row_in[far, 1, 2 * c : 2 * c + 1, lanes]
         send(message)
 
     spans = {0: [(x, x + 2) for x in range(X)], 1: [(X - 2, 0), (X - 1, 1)], -1: [(0, X + 2), (1, X + 3)]}
@@ -215,7 +229,7 @@
             else:
                 parts = [
                     pltpu.roll(
-                        pass_col_in[n, side, g // per_tile],
+                        pass_in[n, cols_at + side * col_tiles + g // per_tile],
                         (first_lane[dx] - wide_lanes * (g % per_tile)) % LANE, 1,
                     )
                     for g in range(groups)
@@ -226,16 +240,20 @@
         for x, here in spans[dx]:
             far = here in (0, X + 3)
             for c in range(3 if far else 4):
-                if far:
-                    high, low = pass_row_in[n, 2, 4 + c : 5 + c], pass_row_in[n, 2, c : c + 1]
-                elif dx == 0:
-                    high, low = row_in[x, 1, 2 * c : 2 * c + 2], row_in[x, 0, 2 * c : 2 * c + 2]
-                else:
-                    high, low = pass_row_in[n, 1, 2 * c : 2 * c + 2], pass_row_in[n, 0, 2 * c : 2 * c + 2]
-                high = jnp.where(high_open, high, 0.0)
-                low = jnp.where(low_open, low, 0.0)
-                gap = jnp.zeros((SUB - 2 * high.shape[0], Z), jnp.float32)
-                ext[c, here, Y:YE, 0:Z] = jnp.concatenate([high, gap, low], 0)
+                for z, lanes in enumerate(lanes_of):
+                    if far:
+                        high, low = pass_in[n, 3 * z + 2, 4 + c : 5 + c], pass_in[n, 3 * z + 2, c : c + 1]
+                    elif dx == 0:
+                        high, low = (row_in[x, side, 2 * c : 2 * c + 2, lanes] for side in (1, 0))
+                    else:
+                        high, low = (pass_in[n, 3 * z + side, 2 * c : 2 * c + 2] for side in (1, 0))
+                    high = jnp.where(high_open, high, 0.0)
+                    low = jnp.where(low_open, low, 0.0)
+                    gap = jnp.zeros((SUB - 2 * high.shape[0], LANE), jnp.float32)
+                    ext[c, here, Y:YE, lanes] = jnp.concatenate([high, gap, low], 0)
+                    if c == 3 and dx != 0:
+                        for y in range(Y // SUB):
+                            ext[c, here, y * SUB : (y + 1) * SUB, lanes] = pass_in[n, visc_at + z * (Y // SUB) + y]
                 ext[c, here, :, Z:ZE] = pltpu.roll(whole, LANE - 4 * (x * 4 + c) - 2, 1)
 
     unpack(0)
@@ -271,7 +289,7 @@
     arrive(planes + passed)
     unpack(1)
     unpack(-1)
-    lax.fori_loop(0, 4, lambda n, carry: flow(n + (n // 2) * (X - 2), carry), 0)
+    lax.fori_loop(0, 4, lambda n, carry: flow(jnp.where(n < 2, n, n + (X - 2)), carry), 0)
 
     arrive(seeds)
     seed_all[...] = seed_in[...]
@@ -357,6 +375,7 @@
     vmem = pl.BlockSpec(memory_space=pltpu.VMEM)
     hbm = pl.BlockSpec(memory_space=pltpu.HBM)
     f32, i32 = jnp.float32, jnp.int32
+    pass_tiles = (Z // LANE) * (3 + Y // SUB) + len(sides) * -(-(Y // SUB + 2) // 4)
     shifted, seed_all = pl.pallas_call(
         functools.partial(exchange, sizes),
         out_shape=(
@@ -374,10 +393,8 @@
             pltpu.VMEM((2, X, SUB, Z), f32),
             pltpu.VMEM((len(sides), Y + 2 * SUB, LANE), f32),
             pltpu.VMEM((X, 2, SUB, Z), f32),
-            pltpu.VMEM((2, len(sides), -(-(Y // SUB + 2) // 4), SUB, LANE), f32),
-            pltpu.VMEM((2, len(sides), -(-(Y // SUB + 2) // 4), SUB, LANE), f32),
-            pltpu.VMEM((2, 3, SUB, Z), f32),
-            pltpu.VMEM((2, 3, SUB, Z), f32),
+            pltpu.VMEM((2, pass_tiles, SUB, LANE), f32),
+            pltpu.VMEM((2, pass_tiles, SUB, LANE), f32),
             pltpu.VMEM((n_tile, 4 * CAP, n_pts), i32),
             pltpu.VMEM((n_tile, 4 * CAP, n_pts), i32),
             pltpu.SemaphoreType.DMA((total,)),

time: 16.6 us -> 16.7 us (level)
  no operation moved by 1% of the time
where the time goes in v6:
time: 16.7 us; the launch traced here: 16.6 us
  Pallas kernels  15.3 us (92%)
  between operations  1.28 us (8%)
    pallas_call x1, Pallas kernels, shards(): pl.pallas_call(functools.partial(exchange, sizes), out_shape=(jax.ShapeDt...  13.6 us
    pallas_call x1, Pallas kernels, shards(): pl.pallas_call(pathlines, out_shape=(jax.ShapeDtypeStruct((3, X, Y, Z), f...  1.7 us

profile of v6, /device:TPU:0, one launch (start us, length us, event | category | flops | bytes accessed | tf_op | source)
XLA Modules:
  0.0 16.6 jit_solution(3955361344687146055)
XLA Ops:
  1.3 13.6 %shard_map.77 = (f32[3,3,3,6,16,128]{5,4,3,2,1,0:T(8,128)S(1)}, s32[4,8,128]{2,1,0:T(8,128)S(1)}) custom-call(s32[1,1,1]{2,1,0:T(1,128)S(6)} %copy.8.counts_ref, s32[1,1,1,4]{3,2,1,0:T(1,128)} %dest_hbm.1, f32[3,4,16,128]{3,2,1,0:T(8,128)} %vel_hbm.1, f32[4,16,128]{2,1,0:T(8,128)} %visc_hbm.1, s32[3,4,128]{2,1,0:T(4,128)} %bitcast.7, s32[4,128]{1,0:T(4,128)} %bitcast.8), custom_call_target="tpu_custom_call" | custom-call | tf_op jit(solution)/shard_map/pallas_call | solution.py:379
  14.9 1.7 %shard_map.78 = (f32[3,4,16,128]{3,2,1,0:T(8,128)}, f32[3,8,128]{2,1,0:T(8,128)}) custom-call(f32[3,3,3,6,16,128]{5,4,3,2,1,0:T(8,128)S(1)} %get-tuple-element.6.shifted, s32[4,8,128]{2,1,0:T(8,128)S(1)} %get-tuple-element.7.seed_all), custom_call_target="tpu_custom_call" | custom-call | tf_op jit(solution)/shard_map/pallas_call | solution.py:415

commit v7 on v6

--- a/solution.py
+++ b/solution.py
@@ -92,7 +92,7 @@
 
     copies = {}
 
-    def send(message):
+    def prepare(message):
         kind, dx, dy, dz = message
         m = messages.index(message)
         if kind == "seed":
@@ -118,14 +118,30 @@
             device_id=device(dx, dy, dz), device_id_type=MESH,
         )
         copies[message] = copy
-        guarded(allowed(kind, dy)[0], copy.start)
+
+    def send(message):
+        prepare(message)
+        guarded(allowed(message[0], message[2])[0], copies[message].start)
+
+    def send_wide(group):
+        for message in group:
+            prepare(message)
+
+        @pl.when(w == n_wide - 1)
+        def _():
+            for message in reversed(group):
+                copies[message].start()
+
+        @pl.when(w != n_wide - 1)
+        def _():
+            for message in group:
+                copies[message].start()
 
     def arrive(group):
         for message in group:
             guarded(allowed(message[0], message[2])[1], copies[message].wait_recv)
 
-    for message in planes:
-        send(message)
+    send_wide(planes)
 
     loads[0].wait()
     loads[1].wait()
@@ -214,7 +230,7 @@
             for c in range(4):
                 pass_out[n, 3 * z + 2, c : c + 1] = row_in[far, 0, 2 * c + 1 : 2 * c + 2, lanes]
                 pass_out[n, 3 * z + 2, 4 + c : 5 + c] = row_in[far, 1, 2 * c : 2 * c + 1, lanes]
-        send(message)
+    send_wide(passed)
 
     spans = {0: [(x, x + 2) for x in range(X)], 1: [(X - 2, 0), (X - 1, 1)], -1: [(0, X + 2), (1, X + 3)]}
     keep8 = ((sub8 < SUB // 2) & high_open) | ((sub8 >= SUB // 2) & low_open)
@@ -286,11 +302,18 @@
         return carry
 
     lax.fori_loop(2, X, flow, 0)
-    arrive(planes + passed)
-    unpack(1)
-    unpack(-1)
-    lax.fori_loop(0, 4, lambda n, carry: flow(jnp.where(n < 2, n, n + (X - 2)), carry), 0)
-
+
+    def take(dx):
+        arrive([message for message in planes + passed if message[1] == dx])
+        unpack(dx)
+
+    pl.when(w != 0)(lambda: take(1))
+    pl.when(w == 0)(lambda: take(-1))
+    base = jnp.where(w == 0, X, 0)
+    lax.fori_loop(0, 2, lambda n, carry: flow(base + n, carry), 0)
+    pl.when(w != 0)(lambda: take(-1))
+    pl.when(w == 0)(lambda: take(1))
+    lax.fori_loop(0, 2, lambda n, carry: flow(X - base + n, carry), 0)
     arrive(seeds)
     seed_all[...] = seed_in[...]
     for message in messages:

time: 16.7 us -> 15.9 us (0.952)
  Pallas kernels: 15.3 us -> 14.5 us
    pallas_call x1, Pallas kernels: 13.6 us -> 12.8 us  [shards(): pl.pallas_call(functools.partial(exchange, sizes), out_shape=(jax.ShapeDt...]
where the time goes in v7:
time: 15.9 us; the launch traced here: 15.8 us
  Pallas kernels  14.5 us (91%)
  between operations  1.28 us (8%)
    pallas_call x1, Pallas kernels, shards(): pl.pallas_call(functools.partial(exchange, sizes), out_shape=(jax.ShapeDt...  12.8 us
    pallas_call x1, Pallas kernels, shards(): pl.pallas_call(pathlines, out_shape=(jax.ShapeDtypeStruct((3, X, Y, Z), f...  1.7 us

profile of v7, /device:TPU:0, one launch (start us, length us, event | category | flops | bytes accessed | tf_op | source)
XLA Modules:
  0.0 15.8 jit_solution(15858630294590579520)
XLA Ops:
  1.3 12.8 %shard_map.77 = (f32[3,3,3,6,16,128]{5,4,3,2,1,0:T(8,128)S(1)}, s32[4,8,128]{2,1,0:T(8,128)S(1)}) custom-call(s32[1,1,1]{2,1,0:T(1,128)S(6)} %copy.8.counts_ref, s32[1,1,1,4]{3,2,1,0:T(1,128)} %dest_hbm.1, f32[3,4,16,128]{3,2,1,0:T(8,128)} %vel_hbm.1, f32[4,16,128]{2,1,0:T(8,128)} %visc_hbm.1, s32[3,4,128]{2,1,0:T(4,128)} %bitcast.7, s32[4,128]{1,0:T(4,128)} %bitcast.8), custom_call_target="tpu_custom_call" | custom-call | tf_op jit(solution)/shard_map/pallas_call | solution.py:402
  14.1 1.7 %shard_map.78 = (f32[3,4,16,128]{3,2,1,0:T(8,128)}, f32[3,8,128]{2,1,0:T(8,128)}) custom-call(f32[3,3,3,6,16,128]{5,4,3,2,1,0:T(8,128)S(1)} %get-tuple-element.6.shifted, s32[4,8,128]{2,1,0:T(8,128)S(1)} %get-tuple-element.7.seed_all), custom_call_target="tpu_custom_call" | custom-call | tf_op jit(solution)/shard_map/pallas_call | solution.py:438

commit v8 on v7

--- a/solution.py
+++ b/solution.py
@@ -31,8 +31,8 @@
 def exchange(
     sizes,
     counts_ref, dest_hbm, vel_hbm, visc_hbm, seeds_hbm, steps_hbm,
-    shifted, seed_all,
-    ext, dest_ref, seeds_ref, steps_ref,
+    new_ref, dense, seed_all,
+    ext, shifted, dest_ref, seeds_ref, steps_ref,
     col_out, row_out, col_in, row_in, pass_out, pass_in, seed_out, seed_in,
     send_sem, recv_sem, load_sem,
 ):
@@ -303,33 +303,6 @@
 
     lax.fori_loop(2, X, flow, 0)
 
-    def take(dx):
-        arrive([message for message in planes + passed if message[1] == dx])
-        unpack(dx)
-
-    pl.when(w != 0)(lambda: take(1))
-    pl.when(w == 0)(lambda: take(-1))
-    base = jnp.where(w == 0, X, 0)
-    lax.fori_loop(0, 2, lambda n, carry: flow(base + n, carry), 0)
-    pl.when(w != 0)(lambda: take(-1))
-    pl.when(w == 0)(lambda: take(1))
-    lax.fori_loop(0, 2, lambda n, carry: flow(X - base + n, carry), 0)
-    arrive(seeds)
-    seed_all[...] = seed_in[...]
-    for message in messages:
-        guarded(allowed(message[0], message[2])[0], copies[message].wait_send)
-
-
-def pathlines(shifted, seed_all, new_hbm, out_hbm, dense, out_ref, new_sem, out_sem):
-    _, _, _, planes, Y, Z = shifted.shape
-    X = planes - 2
-    writes = [
-        pltpu.make_async_copy(shifted.at[1, 1, c, 1 : X + 1], new_hbm.at[c], new_sem.at[c])
-        for c in range(3)
-    ]
-    for write in writes:
-        write.start()
-
     def hat(e):
         return (jnp.maximum(-e, 0.0), 1.0 - jnp.abs(e), jnp.maximum(e, 0.0))
 
@@ -358,10 +331,35 @@
         k3 = sample([0.5 * trace_step * k for k in k2])
         k4 = sample([trace_step * k for k in k3])
         for c in range(3):
+            new_ref[c, i] = k1[c]
             dense[c, i] = trace_step / 6.0 * (k1[c] + 2.0 * k2[c] + 2.0 * k3[c] + k4[c])
         return carry
 
-    lax.fori_loop(0, X, trace, 0)
+    def take(dx):
+        arrive([message for message in planes + passed if message[1] == dx])
+        unpack(dx)
+
+    pl.when(w != 0)(lambda: take(1))
+    pl.when(w == 0)(lambda: take(-1))
+    base = jnp.where(w == 0, X, 0)
+    lax.fori_loop(0, 2, lambda n, carry: flow(base + n, carry), 0)
+    early = jnp.where(w == 0, 2, 0)
+    lax.fori_loop(0, X - 2, lambda n, carry: trace(early + n, carry), 0)
+    pl.when(w != 0)(lambda: take(-1))
+    pl.when(w == 0)(lambda: take(1))
+    lax.fori_loop(0, 2, lambda n, carry: flow(X - base + n, carry), 0)
+    late = jnp.where(w == 0, 0, X - 2)
+    lax.fori_loop(0, 2, lambda n, carry: trace(late + n, carry), 0)
+    arrive(seeds)
+    seed_all[...] = seed_in[...]
+    for message in messages:
+        guarded(allowed(message[0], message[2])[0], copies[message].wait_send)
+
+
+def lookup(new_ref, dense, seed_all, new_hbm, out_hbm, out_ref, new_sem, out_sem):
+    _, X, Y, Z = dense.shape
+    new_write = pltpu.make_async_copy(new_ref, new_hbm, new_sem)
+    new_write.start()
 
     sub = lax.broadcasted_iota(jnp.int32, (SUB, LANE), 0)
     for d in range(seed_all.shape[0]):
@@ -384,8 +382,7 @@
                 out_ref[c, slot : slot + 1] = jnp.sum(found, 0, keepdims=True)
     write = pltpu.make_async_copy(out_ref, out_hbm, out_sem)
     write.start()
-    for other in writes:
-        other.wait()
+    new_write.wait()
     write.wait()
 
 
@@ -399,16 +396,18 @@
     hbm = pl.BlockSpec(memory_space=pltpu.HBM)
     f32, i32 = jnp.float32, jnp.int32
     pass_tiles = (Z // LANE) * (3 + Y // SUB) + len(sides) * -(-(Y // SUB + 2) // 4)
-    shifted, seed_all = pl.pallas_call(
+    new, dense, seed_all = pl.pallas_call(
         functools.partial(exchange, sizes),
         out_shape=(
-            jax.ShapeDtypeStruct((3, 3, 3, X + 2, Y, Z), f32),
+            jax.ShapeDtypeStruct((3, X, Y, Z), f32),
+            jax.ShapeDtypeStruct((3, X, Y, Z), f32),
             jax.ShapeDtypeStruct((n_tile, 4 * CAP, n_pts), i32),
         ),
         in_specs=[pl.BlockSpec(memory_space=pltpu.SMEM)] + [hbm] * 5,
-        out_specs=(vmem, vmem),
+        out_specs=(vmem, vmem, vmem),
         scratch_shapes=[
             pltpu.VMEM((4, X + 4, Y + SUB, Z + LANE), f32),
+            pltpu.VMEM((3, 3, 3, X + 2, Y, Z), f32),
             pltpu.SMEM(destination.shape, i32),
             pltpu.VMEM((3, n_blk, n_pts), i32),
             pltpu.VMEM((n_blk, n_pts), i32),
@@ -436,21 +435,20 @@
     )
     slots = n_tile * CAP
     fresh, result = pl.pallas_call(
-        pathlines,
+        lookup,
         out_shape=(
             jax.ShapeDtypeStruct((3, X, Y, Z), f32),
             jax.ShapeDtypeStruct((3, slots, n_pts), f32),
         ),
-        in_specs=[vmem, vmem],
+        in_specs=[vmem, vmem, vmem],
         out_specs=(hbm, hbm),
         scratch_shapes=[
-            pltpu.VMEM((3, X, Y, Z), f32),
             pltpu.VMEM((3, slots, n_pts), f32),
-            pltpu.SemaphoreType.DMA((3,)),
+            pltpu.SemaphoreType.DMA,
             pltpu.SemaphoreType.DMA,
         ],
         compiler_params=pltpu.CompilerParams(vmem_limit_bytes=16 * 2**20),
-    )(shifted, seed_all)
+    )(new, dense, seed_all)
     return fresh, jnp.transpose(result, (1, 0, 2))[None, None, None]
 
 

time: 15.9 us -> 15.5 us (0.975)
  Pallas kernels: 14.5 us -> 14.1 us
    pallas_call x1, Pallas kernels: 1.7 us -> 0.92 us  [shards(): pl.pallas_call(lookup, out_shape=(jax.ShapeDtypeStruct((3, X, Y, Z), f32)...]
    pallas_call x1, Pallas kernels: 12.8 us -> 13.2 us  [shards(): pl.pallas_call(functools.partial(exchange, sizes), out_shape=(jax.ShapeDt...]
where the time goes in v8:
time: 15.5 us; the launch traced here: 15.4 us
  Pallas kernels  14.1 us (91%)
  between operations  1.28 us (8%)
    pallas_call x1, Pallas kernels, shards(): pl.pallas_call(functools.partial(exchange, sizes), out_shape=(jax.ShapeDt...  13.2 us
    pallas_call x1, Pallas kernels, shards(): pl.pallas_call(lookup, out_shape=(jax.ShapeDtypeStruct((3, X, Y, Z), f32)...  0.92 us

profile of v8, /device:TPU:0, one launch (start us, length us, event | category | flops | bytes accessed | tf_op | source)
XLA Modules:
  0.0 15.4 jit_solution(1640616324775963699)
XLA Ops:
  1.3 13.2 %shard_map.77 = (f32[3,4,16,128]{3,2,1,0:T(8,128)S(1)}, f32[3,4,16,128]{3,2,1,0:T(8,128)S(1)}, s32[4,8,128]{2,1,0:T(8,128)S(1)}) custom-call(s32[1,1,1]{2,1,0:T(1,128)S(6)} %copy.8.counts_ref, s32[1,1,1,4]{3,2,1,0:T(1,128)} %dest_hbm.1, f32[3,4,16,128]{3,2,1,0:T(8,128)} %vel_hbm.1, f32[4,16,128]{2,1,0:T(8,128)} %visc_hbm.1, s32[3,4,128]{2,1,0:T(4,128)} %bitcast.7, ...), custom_call_target="tpu_custom_call" | custom-call | tf_op jit(solution)/shard_map/pallas_call | solution.py:399
  14.5 0.9 %shard_map.78 = (f32[3,4,16,128]{3,2,1,0:T(8,128)}, f32[3,8,128]{2,1,0:T(8,128)}) custom-call(f32[3,4,16,128]{3,2,1,0:T(8,128)S(1)} %get-tuple-element.7.new_ref, f32[3,4,16,128]{3,2,1,0:T(8,128)S(1)} %get-tuple-element.8.dense, s32[4,8,128]{2,1,0:T(8,128)S(1)} %get-tuple-element.9.seed_all), custom_call_target="tpu_custom_call" | custom-call | tf_op jit(solution)/shard_map/pallas_call | solution.py:437

commit v9 on v8

--- a/solution.py
+++ b/solution.py
@@ -339,16 +339,17 @@
         arrive([message for message in planes + passed if message[1] == dx])
         unpack(dx)
 
-    pl.when(w != 0)(lambda: take(1))
-    pl.when(w == 0)(lambda: take(-1))
-    base = jnp.where(w == 0, X, 0)
+    high_first = w < n_wide // 2
+    pl.when(jnp.logical_not(high_first))(lambda: take(1))
+    pl.when(high_first)(lambda: take(-1))
+    base = jnp.where(high_first, X, 0)
     lax.fori_loop(0, 2, lambda n, carry: flow(base + n, carry), 0)
-    early = jnp.where(w == 0, 2, 0)
+    early = jnp.where(high_first, 2, 0)
     lax.fori_loop(0, X - 2, lambda n, carry: trace(early + n, carry), 0)
-    pl.when(w != 0)(lambda: take(-1))
-    pl.when(w == 0)(lambda: take(1))
+    pl.when(jnp.logical_not(high_first))(lambda: take(-1))
+    pl.when(high_first)(lambda: take(1))
     lax.fori_loop(0, 2, lambda n, carry: flow(X - base + n, carry), 0)
-    late = jnp.where(w == 0, 0, X - 2)
+    late = jnp.where(high_first, 0, X - 2)
     lax.fori_loop(0, 2, lambda n, carry: trace(late + n, carry), 0)
     arrive(seeds)
     seed_all[...] = seed_in[...]

time: 15.5 us -> 15.5 us (level)
  no operation moved by 1% of the time
where the time goes in v9:
time: 15.5 us; the launch traced here: 15.4 us
  Pallas kernels  14.1 us (91%)
  between operations  1.28 us (8%)
    pallas_call x1, Pallas kernels, shards(): pl.pallas_call(functools.partial(exchange, sizes), out_shape=(jax.ShapeDt...  13.2 us
    pallas_call x1, Pallas kernels, shards(): pl.pallas_call(lookup, out_shape=(jax.ShapeDtypeStruct((3, X, Y, Z), f32)...  0.92 us

profile of v9, /device:TPU:0, one launch (start us, length us, event | category | flops | bytes accessed | tf_op | source)
XLA Modules:
  0.0 15.4 jit_solution(11922753487811214259)
XLA Ops:
  1.3 13.2 %shard_map.77 = (f32[3,4,16,128]{3,2,1,0:T(8,128)S(1)}, f32[3,4,16,128]{3,2,1,0:T(8,128)S(1)}, s32[4,8,128]{2,1,0:T(8,128)S(1)}) custom-call(s32[1,1,1]{2,1,0:T(1,128)S(6)} %copy.8.counts_ref, s32[1,1,1,4]{3,2,1,0:T(1,128)} %dest_hbm.1, f32[3,4,16,128]{3,2,1,0:T(8,128)} %vel_hbm.1, f32[4,16,128]{2,1,0:T(8,128)} %visc_hbm.1, s32[3,4,128]{2,1,0:T(4,128)} %bitcast.7, ...), custom_call_target="tpu_custom_call" | custom-call | tf_op jit(solution)/shard_map/pallas_call | solution.py:400
  14.5 0.9 %shard_map.78 = (f32[3,4,16,128]{3,2,1,0:T(8,128)}, f32[3,8,128]{2,1,0:T(8,128)}) custom-call(f32[3,4,16,128]{3,2,1,0:T(8,128)S(1)} %get-tuple-element.7.new_ref, f32[3,4,16,128]{3,2,1,0:T(8,128)S(1)} %get-tuple-element.8.dense, s32[4,8,128]{2,1,0:T(8,128)S(1)} %get-tuple-element.9.seed_all), custom_call_target="tpu_custom_call" | custom-call | tf_op jit(solution)/shard_map/pallas_call | solution.py:438
